TPU v7x, 128 devices: a whole 4x4x4 slice. The times are simulated.
128 devices in a mesh: ctx: 8 (over x, z_lo), head: 16 (over z_hi, y, core).
Axes of the slice: x: 4, y: 4, z: 4 (z_hi: 2, z_lo: 2; z = z_hi * 2 + z_lo), core: 2. Of those that a mesh axis runs over, the one named last changes fastest.
Arguments:
- queries: bfloat16 [4096, 24576], P('ctx', 'head'), may hold values from -300 to 300
- latents: bfloat16 [4096, 576], P('ctx'), may hold values from -1000 to 1000
- block_order: int32 [16], replicated, may hold values from 0 to 15, each once
- norm_gain: float32 [512], replicated, may hold values from 0.1 to 1.9
- w_kv_up: bfloat16 [512, 32768], P(None, 'head'), may hold values from -0.25 to 0.25
- w_out: bfloat16 [16384, 7168], P('head', 'ctx'), may hold values from -0.046875 to 0.046875
Outputs:
- mixed: bfloat16 [4096, 7168], P(('ctx', 'head'))
Inputs may be any that keep to these rules, and one draw needn't show every extreme that they name: `block_order`: each block of 0 to 2 * 8 - 1 stands in exactly one slot.
All inputs are finite; a program needn't handle non-finite values.
Results may differ from a plain program's by a relative error of at most 0.02.
Values may be sent and summed in bfloat16 or wider, within the bound.
No kernel may reach another device: no remote copies, remote signals or barrier semaphores. Data moves between devices by JAX's collectives and lax.ppermute only.
A program may use at most 320 MiB of HBM per device.

v0:
```python
import jax
import jax.numpy as jnp
from jax import lax
from jax.sharding import PartitionSpec as P

KV_RANK = 512
ROPE = 64
PLAIN_PART_SIZE = 128
VHEAD = 128


def position_of(block_order, row_total, block_len):
    row_index = jnp.arange(row_total, dtype=jnp.int32)
    return block_order[row_index // block_len] * block_len + row_index % block_len


def normalize(latents, norm_gain):
    compressed = latents[:, :KV_RANK].astype(jnp.float32)
    mean_square = jnp.mean(compressed * compressed, axis=-1, keepdims=True)
    return (compressed * lax.rsqrt(mean_square + 1e-06) * norm_gain).astype(jnp.bfloat16)


def on_device(queries, latents, block_order, norm_gain, w_kv_up, w_out):
    tok_dev = queries.shape[0]
    block_len = tok_dev // 2
    ctx_count = lax.axis_size("ctx")
    total_rows = tok_dev * ctx_count
    head_local = w_kv_up.shape[1] // (PLAIN_PART_SIZE + VHEAD)
    packed = jnp.concatenate([normalize(latents, norm_gain), latents[:, KV_RANK:]], axis=1)
    gathered = lax.all_gather(packed, "ctx", axis=0, tiled=True)
    normed_all = gathered[:, :KV_RANK]
    rope_keys = gathered[:, KV_RANK:]
    key_pos = position_of(block_order, total_rows, block_len)
    query_pos = lax.dynamic_slice_in_dim(key_pos, lax.axis_index("ctx") * tok_dev, tok_dev)
    visible = key_pos[None, :] <= query_pos[:, None]
    query_heads = queries.reshape(tok_dev, head_local, PLAIN_PART_SIZE + ROPE)
    weight_heads = w_kv_up.reshape(KV_RANK, head_local, PLAIN_PART_SIZE + VHEAD)
    w_key = weight_heads[..., :PLAIN_PART_SIZE]
    w_value = weight_heads[..., PLAIN_PART_SIZE:]
    logits = jnp.einsum(
        "qhd,td->qht",
        query_heads[..., PLAIN_PART_SIZE:],
        rope_keys,
        preferred_element_type=jnp.float32,
    )
    keys_nope = jnp.einsum(
        "tr,rhd->thd", normed_all, w_key, preferred_element_type=jnp.float32
    ).astype(jnp.bfloat16)
    logits = logits + jnp.einsum(
        "qhd,thd->qht",
        query_heads[..., :PLAIN_PART_SIZE],
        keys_nope,
        preferred_element_type=jnp.float32,
    )
    score_scale = 1.0 / (PLAIN_PART_SIZE + ROPE) ** 0.5
    logits = jnp.where(visible[:, None, :], logits * score_scale, -jnp.inf)
    peak = jnp.max(logits, axis=-1, keepdims=True)
    expo = jnp.exp(logits - peak)
    probs = (expo / jnp.sum(expo, axis=-1, keepdims=True)).astype(jnp.bfloat16)
    values = jnp.einsum(
        "tr,rhd->thd", normed_all, w_value, preferred_element_type=jnp.float32
    ).astype(jnp.bfloat16)
    context = jnp.einsum("qht,thd->qhd", probs, values, preferred_element_type=jnp.float32)
    attention = context.reshape(tok_dev, head_local * VHEAD).astype(jnp.bfloat16)
    partial_sums = jnp.dot(
        attention,
        lax.all_gather(w_out, "ctx", axis=1, tiled=True),
        preferred_element_type=jnp.float32,
    )
    return lax.psum_scatter(
        partial_sums.astype(jnp.bfloat16), "head", scatter_dimension=0, tiled=True
    )


def solution(mesh):
    in_specs = (P("ctx", "head"), P("ctx", None), P(), P(), P(None, "head"), P("head", "ctx"))
    out_specs = P(("ctx", "head"), None)
    return jax.shard_map(
        on_device, mesh=mesh, in_specs=in_specs, out_specs=out_specs, check_vma=False
    )
```

profile of v0, /device:TPU:0, one launch (start us, length us, event | category | flops | bytes accessed | tf_op | source)
XLA Modules:
  0.0 519.1 jit_solution(11761037460135071039)
XLA Ops:
  6.5 1.2 fusion.12
  7.7 0.8 slice.25
  8.6 1.2 fusion.14
  9.8 0.9 pad_maximum_fusion
  10.7 0.7 all-gather.5.cloned.1.call-update
  11.5 2.6 copy.10
  14.1 2.3 copy.17
  16.4 0.1 compare_reduce_fusion
  16.6 0.1 compare_reduce_fusion.3
  16.8 0.1 compare_reduce_fusion.7
  16.9 0.7 fusion.27
  17.6 4.3 compare_select_fusion.1
  22.0 5.8 %fusion.22 = s32[4096]{0:T(1024)S(1)} fusion(pred[4096]{0:T(1024)(128)(4,1)S(1)} %compare_reduce_fusion, pred[4096]{0:T(1024)(128)(4,1)S(1)} %compare_reduce_fusion.1, pred[4096]{0:T(1024)(128)(4,1)S(1)} %compare_reduce_fusion.2, pred[4096]{0:T(1024)(128)(4,1)S(1)} %compare_reduce_fusion.3, pred[4096]{0:T(1024)(128)(4,1)S(1)} %compare_reduce_fusion.4, ...), kind=kLoop, calls=%fused_computation.48 | loop fusion | flops 69632 | bytes 69668 | tf_op jit(solution)/shard_map/add | solution.py:14
  27.7 0.1 dynamic_slice.3
  27.8 1.1 fusion.26
  29.0 1.9 broadcast_compare_fusion
  30.9 82.1 %all-gather.3.cloned.1.call-done = bf16[4096,576]{0,1:T(8,128)(2,1)} async-done(((bf16[512,576]{0,1:T(8,128)(2,1)}), bf16[4096,576]{0,1:T(8,128)(2,1)}) %all-gather.3.cloned.1.call-update) | async-done | bytes 4718608 | tf_op jit(solution)/shard_map/all_gather | solution.py:30
  112.9 26.0 %fusion.20 = f32[4096,512,8]{1,0,2:T(8,128)} fusion(bf16[512,8,192]{0,2,1:T(8,128)(2,1)} %bitcast.56, bf16[4096,576]{0,1:T(8,128)(2,1)} %all-gather.3.cloned.1.call-done), kind=kOutput, calls=%fused_computation.24 | convolution fusion | flops 2147483648 | bytes 68157440 | tf_op jit(solution)/shard_map/qhd,td->qht/dot_general | solution.py:40
  138.9 46.5 %fusion.2 = f32[512,8,4096]{0,2,1:T(8,128)} fusion(f32[4096,512,8]{1,0,2:T(8,128)} %fusion.20, pred[512,4096]{0,1:T(8,128)(4,1)S(1)} %broadcast_compare_fusion, bf16[4096,576]{0,1:T(8,128)(2,1)} %all-gather.3.cloned.1.call-done, bf16[512,8,192]{0,2,1:T(8,128)(2,1)} %bitcast.57, bf16[512,8,128]{2,1,0:T(8,128)(2,1)S(1)} %get-tuple-element.6), kind=kOutput, calls=%fused_computation.3 | convolution fusion | flops 8644460544 | bytes 142606336 | tf_op jit(solution)/shard_map/qhd,thd->qht/dot_general | solution.py:49
  185.5 66.9 %fusion.28 = (f32[512,8]{0,1:T(8,128)S(1)}, f32[512,8,4096]{0,2,1:T(8,128)}) fusion(f32[512,8,4096]{0,2,1:T(8,128)} %fusion.2), kind=kOutput, calls=%fused_computation.57 | output fusion | flops 33558528 | bytes 134234112 | tf_op jit(solution)/shard_map/sub | solution.py:58
  252.3 25.0 %fusion.9 = bf16[8,128,512]{2,1,0:T(8,128)(2,1)S(1)} fusion(f32[512,8,4096]{0,2,1:T(8,128)} %get-tuple-element.24, f32[512,8]{0,1:T(8,128)S(1)} %get-tuple-element.23, bf16[4096,576]{0,1:T(8,128)(2,1)} %all-gather.3.cloned.1.call-done, bf16[512,8,128]{2,1,0:T(8,128)(2,1)S(1)} %copy-done), kind=kOutput, calls=%fused_computation.14 | convolution fusion | flops 8628207616 | bytes 73416704 | tf_op jit(solution)/shard_map/qht,thd->qhd/dot_general | solution.py:63
  277.3 124.6 %all-gather.5.cloned.1.call-done = bf16[1024,7168]{1,0:T(8,128)(2,1)} async-done(((bf16[1024,896]{1,0:T(8,128)(2,1)}), bf16[1024,7168]{1,0:T(8,128)(2,1)}) %all-gather.5.cloned.1.call-update) | async-done | bytes 14680080 | tf_op jit(solution)/shard_map/all_gather | solution.py:67
  401.9 15.1 %convolution_convert_fusion = bf16[512,7168]{1,0:T(8,128)(2,1)} fusion(bf16[512,1024]{0,1:T(8,128)(2,1)S(1)} %bitcast.60, bf16[1024,7168]{1,0:T(8,128)(2,1)} %all-gather.5.cloned.1.call-done), kind=kOutput, calls=%fused_computation.7 | convolution fusion | flops 7519862784 | bytes 23068672 | tf_op jit(solution)/shard_map/dot_general | solution.py:65
  417.1 95.5 %reduce-scatter.2.cloned.1.call-done = bf16[32,7168]{1,0:T(8,128)(2,1)} async-done(((bf16[512,7168]{1,0:T(8,128)(2,1)}), bf16[32,7168]{1,0:T(8,128)(2,1)}) %reduce-scatter.2.cloned.1.call-update) | async-done | bytes 458768 | tf_op jit(solution)/shard_map/reduce_scatter | solution.py:70
  (16 shorter events, 0.5 us)
Async XLA Ops:
  6.5 10.4 %copy-start.1 = (s32[16]{0:T(128)S(1)}, s32[16]{0:T(128)}, u32[]{:S(2)}) copy-start(s32[16]{0:T(128)} %param.8) | copy-start | bytes 196
  6.5 106.4 %all-gather.3.cloned.1.call-start = ((), (), s32[]{:S(2)}) async-start(), calls=%async_computation.1 | async-start | bytes 5308416 | tf_op jit(solution)/shard_map/all_gather | solution.py:30
  10.7 391.3 %all-gather.5.cloned.1.call-start = ((), (), s32[]{:S(2)}) async-start(), calls=%async_computation.2 | async-start | bytes 16515072 | tf_op jit(solution)/shard_map/all_gather | solution.py:67
  11.4 501.1 %reduce-scatter.2.cloned.1.call-start = ((), (), s32[]{:S(2)}) async-start(), calls=%async_computation.3 | async-start | bytes 7798784 | tf_op jit(solution)/shard_map/reduce_scatter | solution.py:70
  185.5 66.9 %copy-start = (bf16[512,8,128]{2,1,0:T(8,128)(2,1)S(1)}, bf16[512,8,128]{2,1,0:T(8,128)(2,1)}, u32[]{:S(2)}) copy-start(bf16[512,8,128]{2,1,0:T(8,128)(2,1)} %get-tuple-element.5) | copy-start | bytes 3145732
Sparse Core Ops, SparseCore 0:
  10.8 102.0 all-gather.2
  114.6 287.3 all-gather.4
  417.2 95.3 reduce-scatter.1
where the time goes:
time: 520 us; the launch traced here: 519 us
  waiting for transfers between devices  303 us (58%)
  matrix products  113 us (22%)
  other arithmetic  82.6 us (16%)
  between operations  13.2 us (3%)
  local copies, waits for them, and re-layouts  7.67 us (1%)
    all_gather x1, waiting for transfers between devices, on_device(): lax.all_gather(w_out, 'ctx', axis=1, tiled=True)  125 us
    reduce_scatter x1, waiting for transfers between devices, on_device(): lax.psum_scatter(partial_sums.astype(jnp.bfloat16), 'head', scatter_dimen...  95.5 us
    all_gather x1, waiting for transfers between devices, on_device(): gathered = lax.all_gather(packed, 'ctx', axis=0, tiled=True)  82.1 us
    sub x1, other arithmetic, on_device(): expo = jnp.exp(logits - peak)  66.9 us
    dot_general x1, matrix products, on_device(): jnp.einsum('qhd,thd->qht', query_heads[..., :PLAIN_PART_SIZE], keys_nope,...  46.5 us
    dot_general x1, matrix products, on_device(): jnp.einsum('qhd,td->qht', query_heads[..., PLAIN_PART_SIZE:], rope_keys,...  26 us
    dot_general x1, matrix products, on_device(): jnp.einsum('qht,thd->qhd', probs, values, preferred_element_type=jnp.floa...  25 us
    dot_general x1, matrix products, on_device(): jnp.dot(attention, lax.all_gather(w_out, 'ctx', axis=1, tiled=True), pref...  15.1 us
  transfers between devices with their start and end apart: 3, of which 3 were waited for; matrix products, arithmetic and copies ran while one was open for 35% of the time, Pallas kernels for 0%

commit v1 on v0

v1 whole, which is shorter than its diff:
```python
import functools

import jax
import jax.numpy as jnp
from jax import lax
from jax.experimental import pallas as pl
from jax.experimental.pallas import tpu as pltpu
from jax.sharding import Mesh, PartitionSpec as P

KV_RANK = 512
ROPE = 64
NOPE = 128
BLOCK = 256
NX, NZ, NY = 4, 2, 4
TOKENS = 4096
PIECE = 128
COLS = 1792
TILE = 512
SCALE = (NOPE + ROPE) ** -0.5 * 1.4426950408889634
F32, BF16 = jnp.float32, jnp.bfloat16
NT = (((1,), (1,)), ((), ()))
VMEM = pl.BlockSpec(memory_space=pltpu.VMEM)
SMEM = pl.BlockSpec(memory_space=pltpu.SMEM)


def shift(a, axis, size, step):
    return lax.ppermute(a, axis, [(i, (i + step) % size) for i in range(size)])


def params(mib):
    return pltpu.CompilerParams(vmem_limit_bytes=mib * 2**20)


def cost(flops, nbytes):
    return pl.CostEstimate(flops=flops, bytes_accessed=nbytes, transcendentals=0)


def kv_kernel(turns, info, order, *refs):
    groups, (w_ref, g_ref) = refs[:4], refs[4:6]
    k_ref, v_ref = refs[-2:]
    x, y, c = info[0], info[2], info[3]
    zeros = jnp.zeros((64, PIECE), BF16)
    for n, ref in enumerate(groups):
        zs = c if n < len(turns) else 1 - c
        ys = lax.rem(y + turns[n % len(turns)], NY)
        wide = []
        for s in range(NX):
            a = ref[s, 0:KV_RANK, :].astype(F32)
            ms = jnp.sum(a * a, axis=0, keepdims=True) * (1.0 / KV_RANK)
            wide.append((a * lax.rsqrt(ms + 1e-06) * g_ref[...]).astype(BF16))
        out = jnp.dot(w_ref[...], jnp.concatenate(wide, axis=1), preferred_element_type=F32)
        for s in range(NX):
            xs = lax.rem(x - s + NX, NX)
            row = order[2 * (2 * xs + zs) + ys // 2] * BLOCK + lax.rem(ys, 2) * PIECE
            at = pl.ds(pl.multiple_of(row, PIECE), PIECE)
            o = out[:, PIECE * s : PIECE * (s + 1)]
            rope = (ref[s, KV_RANK : KV_RANK + ROPE, :].astype(F32) * SCALE).astype(BF16)
            k0 = (o[0:128] * SCALE).astype(BF16)
            k1 = (o[256:384] * SCALE).astype(BF16)
            k_ref[0, :, at] = jnp.concatenate([k0, rope, zeros], axis=0)
            k_ref[1, :, at] = jnp.concatenate([zeros, k1, rope], axis=0)
            v_ref[0, :, at] = o[128:256].astype(BF16)
            v_ref[1, :, at] = o[384:512].astype(BF16)


def keys_values(turns, info, order, groups, weights, gain, before=()):
    ins = 2 + len(groups) + 2
    return pl.pallas_call(
        functools.partial(kv_kernel, turns),
        out_shape=(
            jax.ShapeDtypeStruct((2, 256, TOKENS), BF16),
            jax.ShapeDtypeStruct((2, 128, TOKENS), BF16),
        ),
        in_specs=[SMEM, SMEM] + [VMEM] * (len(groups) + 2 + len(before)),
        out_specs=(VMEM, VMEM),
        input_output_aliases={ins + n: n for n in range(len(before))},
        compiler_params=params(20),
        cost_estimate=cost(3 * 10**9, 5 * 10**6),
        name=f"keys_values_{len(before) // 2}",
    )(info, order, *groups, weights, gain, *before)


def attend_kernel(j, info, order, q0, q1, q2, q3, k_ref, v_ref, keep_ref, give_ref, q_ref, s_ref, peak, total, acc):
    for n in range(2):
        turn = lax.rem(info[0] - (j + n) + NX, NX)
        for s, ref in enumerate((q0, q1, q2, q3)):
            @pl.when(turn == s)
            def _():
                q_ref[512 * n : 512 * (n + 1)] = ref[...]

    @pl.loop(0, 2)
    def _(n):
        pos = [order[2 * (2 * (j + n) + info[1]) + r] for r in range(2)]
        full = [a * BLOCK // TILE for a in pos]

        def logits(i, r, slot):
            at = pl.multiple_of(i * TILE, TILE)
            rows = pl.ds(pl.multiple_of(2 * n * BLOCK, BLOCK) + r * BLOCK, BLOCK)
            for h in range(2):
                q = q_ref[rows, 128 * h : 128 * h + 256]
                s_ref[r, slot, h] = jnp.dot(q, k_ref[h, :, pl.ds(at, TILE)], preferred_element_type=F32)

        def weigh(i, r, slot, masked):
            at = pl.multiple_of(i * TILE, TILE)
            for h in range(2):
                s = s_ref[r, slot, h]
                if masked:
                    ahead = lax.broadcasted_iota(jnp.int32, s.shape, 1) - lax.broadcasted_iota(jnp.int32, s.shape, 0)
                    s = jnp.where(ahead <= pos[r] * BLOCK - at, s, -jnp.inf)
                cols = [s[:, 128 * c : 128 * (c + 1)] for c in range(TILE // 128)]
                top = jnp.max(functools.reduce(jnp.maximum, cols), axis=-1, keepdims=True)
                old = peak[r, h]
                top = jnp.maximum(old, jnp.broadcast_to(top, (BLOCK, 128)))
                keep = jnp.exp2(old - top)
                ps = [jnp.exp2(col - top) for col in cols]
                p = jnp.concatenate([a.astype(BF16) for a in ps], axis=1)
                pv = lax.dot_general(p, v_ref[h, :, pl.ds(at, TILE)], NT, preferred_element_type=F32)
                peak[r, h] = top
                total[r, h] = total[r, h] * keep + functools.reduce(jnp.add, ps)
                acc[r, h] = acc[r, h] * keep + pv

        def two_tiles(i, blocks):
            for r in blocks:
                logits(2 * i + 1, r, 1)
            for r in blocks:
                weigh(2 * i, r, 0, False)
            for r in blocks:
                logits(2 * i + 2, r, 0)
            for r in blocks:
                weigh(2 * i + 1, r, 1, False)

        peak[...] = jnp.full(peak.shape, -1e30, F32)
        total[...] = jnp.zeros(total.shape, F32)
        acc[...] = jnp.zeros(acc.shape, F32)
        for r in range(2):
            logits(0, r, 0)
        shared = jnp.minimum(full[0], full[1]) // 2

        @pl.loop(0, shared)
        def _(i):
            two_tiles(i, (0, 1))

        for r in range(2):

            @pl.loop(shared, full[r] // 2)
            def _(i):
                two_tiles(i, (r,))

            @pl.when(lax.rem(full[r], 2) == 1)
            def _():
                logits(full[r], r, 1)
                weigh(full[r] - 1, r, 0, False)

        for r in range(2):
            weigh(full[r], r, lax.rem(full[r], 2), True)
        for r in range(2):
            for h in range(2):
                norm = jnp.sum(total[r, h], axis=-1, keepdims=True)
                o = (acc[r, h] / norm).astype(BF16)
                for y in range(NY):
                    even, odd = o[64 * y : 64 * y + 32], o[64 * y + 32 : 64 * y + 64]
                    at = pl.multiple_of(128 * y + 64 * n + 32 * r, 32)
                    to = (pl.ds(at, 32), slice(128 * h, 128 * h + 128))
                    keep_ref[to] = jnp.where(info[3] == 0, even, odd)
                    give_ref[to] = jnp.where(info[3] == 0, odd, even)


def attend(j, info, order, qs, k, v):
    half = jax.ShapeDtypeStruct((2 * BLOCK, 256), BF16)
    return pl.pallas_call(
        functools.partial(attend_kernel, j),
        out_shape=(half, half),
        in_specs=[SMEM, SMEM] + [VMEM] * 6,
        out_specs=(VMEM, VMEM),
        scratch_shapes=[pltpu.VMEM((4 * BLOCK, 384), BF16), pltpu.VMEM((2, 2, 2, BLOCK, TILE), F32)]
        + [pltpu.VMEM((2, 2, BLOCK, 128), F32)] * 3,
        compiler_params=params(20),
        cost_estimate=cost(10**10, 7 * 10**6),
        name=f"attend_{j}",
    )(info, order, *qs, k, v)


def project_kernel(split, info, *refs):
    outs = refs[-3:] if split else refs[-1:]
    refs = refs[: -len(outs)]
    ctx, (w_ref, w_far) = refs[:-2], refs[-2:]
    if len(ctx) == 1:
        pieces, starts = [ctx[0][n] for n in range(NX)], [256 * n for n in range(NX)]
    else:
        pieces = [ref[...] for ref in ctx]
        starts = [pl.multiple_of(lax.rem(info[0] - s + NX, NX) * 256, 256) for s in range(NX)]
    left = jnp.concatenate(pieces, axis=1)
    right = jnp.concatenate([ref[pl.ds(at, 256), :] for at in starts for ref in (w_ref, w_far)], axis=0)
    out = jnp.dot(left, right, preferred_element_type=F32).astype(BF16)

    def by_y(ref):
        for y in range(NY):
            ref[y] = out[128 * y : 128 * (y + 1)]

    if not split:
        by_y(outs[0])
        return

    @pl.when(pl.program_id(0) == 0)
    def _():
        by_y(outs[0])

    @pl.when(pl.program_id(0) == 1)
    def _():
        for y in range(NY):
            for n in range(2):
                at, rows = 128 * y + 64 * n, slice(32 * n, 32 * (n + 1))
                low, high = out[at : at + 32], out[at + 32 : at + 64]
                outs[1][y, rows] = jnp.where(info[4] == 0, low, high)
                outs[2][y, rows] = jnp.where(info[4] == 0, high, low)


def project(j, info, ctx, w, w_far, split):
    width = COLS // 2
    whole = [pl.BlockSpec(a.shape, lambda n, rank=a.ndim: (0,) * rank) for a in ctx]
    column = pl.BlockSpec((1024, width), lambda n: (0, n))
    if split:
        shapes = [(NY, 128, width), (NY, 64, width), (NY, 64, width)]
        out_specs = [pl.BlockSpec(a, lambda n, rank=len(a): (0,) * rank) for a in shapes]
    else:
        shapes = [(NY, 128, COLS)]
        out_specs = [pl.BlockSpec((NY, 128, width), lambda n: (0, 0, n))]
    return pl.pallas_call(
        functools.partial(project_kernel, split),
        out_shape=[jax.ShapeDtypeStruct(a, BF16) for a in shapes],
        grid=(2,),
        in_specs=[SMEM] + whole + [column, column],
        out_specs=out_specs,
        compiler_params=params(56),
        cost_estimate=cost(4 * 10**9, 7 * 10**6),
        name=f"project_{j}",
    )(info, *ctx, w, w_far)


def hold(*values):
    return lax.optimization_barrier(values)


def on_device(queries, latents, block_order, norm_gain, w_kv_up, w_out):
    x, zl, zh = lax.axis_index("x"), lax.axis_index("zl"), lax.axis_index("zh")
    y, c = lax.axis_index("y"), lax.axis_index("c")
    info = jnp.stack([x, zl, y, c, zh]).astype(jnp.int32)
    w = lax.all_gather(w_out, "zl", axis=1, tiled=True)

    columns = latents.T

    def across(part, s):
        pairs = []
        for xs in range(NX):
            for zs in range(2):
                for cs in range(2):
                    pairs.append(((xs * 2 + zs) * 2 + cs, (((xs + s) % NX) * 2 + cs) * 2 + zs))
        return lax.ppermute(part, ("x", "zl", "c"), pairs)

    near = lax.dynamic_slice_in_dim(columns, y * PIECE, PIECE, 1)
    opposite = lax.dynamic_slice_in_dim(columns, (y + 2) % NY * PIECE, PIECE, 1)
    both = jnp.stack([near, opposite])
    landed = [across(both, s) for s in range(NX)]
    near = jnp.stack([a[0] for a in landed])
    opposite = jnp.stack([a[1] for a in landed])

    qs = [lax.dynamic_slice_in_dim(queries, (x + s) % NX * 384, 384, 1) for s in range(NX)]
    up = lax.dynamic_slice_in_dim(w_kv_up, x * 512, 512, 1).T
    gain = jnp.broadcast_to(norm_gain[:, None], (KV_RANK, PIECE))
    near, opposite, qs, up, gain = hold(near, opposite, qs, up, gain)
    before, after = shift(near, "y", NY, 1), shift(near, "y", NY, 3)
    qs = [qs[0]] + [shift(qs[s], "x", NX, s) for s in range(1, NX)]
    near_far, opposite_far = shift(near, "c", 2, 1), shift(opposite, "c", 2, 1)
    kv = keys_values((0, 2), info, block_order, (near, opposite, near_far, opposite_far), up, gain)
    before, after, info1, *others = hold(before, after, info, *qs[1:])
    qs = [qs[0]] + others
    before_far, after_far = shift(before, "c", 2, 1), shift(after, "c", 2, 1)
    k, v = keys_values((3, 1), info1, block_order, (before, after, before_far, after_far), up, gain, kv)

    def attention(j, info):
        keep, give = attend(j, info, block_order, qs, k, v)
        return jnp.concatenate([keep, shift(give, "c", 2, 1)], axis=1)

    def add_up(a):
        return jnp.sum(a.astype(F32), axis=0).astype(BF16)

    a0, info2, w = hold(attention(0, info1), info1, w)
    w_far = shift(w, "c", 2, 1)
    g0, a1 = [a0] + [shift(a0, "x", NX, s) for s in (1, 2, 3)], attention(2, info2)
    g0, a1, info3, w_far = hold(g0, a1, info2, w_far)
    g1 = lax.all_gather(a1, "x", axis=0, tiled=False)

    def over_y(a):
        return add_up(lax.all_to_all(a, "y", 0, 0, tiled=True))

    def over_z(keep, give):
        return (keep.astype(F32) + shift(give, "zh", 2, 1).astype(F32)).astype(BF16)

    def halves(a):
        a = a.reshape(2, 2, 32, a.shape[-1])
        pick = lambda n: lax.dynamic_index_in_dim(a, n, 1, keepdims=False)
        return pick(zh), pick(1 - zh)

    (p0,) = project(0, info3, g0, w, w_far, False)
    y0 = lax.all_to_all(p0, "y", 0, 0, tiled=True)
    p0, g1, info4 = hold(p0, g1, info3)
    left, keep, give, y0 = hold(*project(1, info4, [g1], w, w_far, True), y0)
    left, right = over_y(left), over_z(keep, give)
    left, right = over_z(*halves(left)), over_y(right).reshape(2, 32, COLS // 2)
    s0 = over_z(*halves(add_up(y0)))
    total = jnp.concatenate([s0, jnp.concatenate([left, right], axis=2)])
    out = lax.all_to_all(total, "x", 0, 0, tiled=True)
    return out.transpose(1, 0, 2).reshape(32, NX * COLS)


def solution(mesh):
    fine = Mesh(mesh.devices.reshape(NX, NZ, 2, NY, 2), ("x", "zl", "zh", "y", "c"))
    ctx, head = ("x", "zl"), ("zh", "y", "c")
    in_specs = (P(ctx, head), P(ctx, None), P(), P(), P(None, head), P(head, ctx))
    return jax.shard_map(
        on_device, mesh=fine, in_specs=in_specs, out_specs=P(ctx + head, None), check_vma=False
    )
```

time: 520 us -> 197 us (0.38)
  waiting for transfers between devices: 303 us -> 65.9 us
  matrix products: 113 us -> 0 us
  other arithmetic: 82.6 us -> 9.64 us
  Pallas kernels: 0 us -> 46.2 us
  starting transfers between devices: 0.08 us -> 34.6 us
  blocking collectives: 0 us -> 10.6 us
  local copies, waits for them, and re-layouts: 7.67 us -> 15.9 us
    all_gather x2, waiting for transfers between devices: 207 us -> 20.3 us  [the longest x1 20.3 us: on_device(): g1 = lax.all_gather(a1, 'x', axis=0, tiled=False)]
    dot_general x4 -> x0, matrix products: 113 us -> none  [the longest x1 46.5 us: on_device(): jnp.einsum('qhd,thd->qht', query_heads[..., :PLAIN_PART_SIZE], keys_nope,...]
    reduce_scatter x1 -> x0, waiting for transfers between devices: 95.5 us -> none  [on_device(): lax.psum_scatter(partial_sums.astype(jnp.bfloat16), 'head', scatter_dimen...]
    sub x1 -> x0, other arithmetic: 66.9 us -> none  [on_device(): expo = jnp.exp(logits - peak)]
    pallas_call x0 -> x6, Pallas kernels: none -> 46.2 us  [the longest x2 22.1 us: attend(): pl.pallas_call(functools.partial(attend_kernel, j), out_shape=(half, half...]
    ppermute x0 -> x22, waiting for transfers between devices: none -> 36.7 us  [the longest x18 27.5 us: shift(): return lax.ppermute(a, axis, [(i, (i + step) % size) for i in range(size)])]
    ppermute x0 -> x22, starting transfers between devices: none -> 21.7 us  [the longest x18 16.4 us: shift(): return lax.ppermute(a, axis, [(i, (i + step) % size) for i in range(size)])]
    all_to_all x0 -> x3, starting transfers between devices: none -> 12.9 us  [the longest x2 8.41 us: over_y(): return add_up(lax.all_to_all(a, 'y', 0, 0, tiled=True))]
  transfers between devices with their start and end apart: 3 -> 27, of which waited for: 3 -> 13; matrix products, arithmetic and copies ran while one was open for 35% -> 8% of each run, Pallas kernels for 0% -> 23%
where the time goes in v1:
time: 197 us
  waiting for transfers between devices  65.9 us (33%)
  Pallas kernels  46.2 us (23%)
  starting transfers between devices  34.6 us (18%)
  local copies, waits for them, and re-layouts  15.9 us (8%)
  between operations  13.8 us (7%)
  blocking collectives  10.6 us (5%)
  other arithmetic  9.64 us (5%)
    ppermute x18, waiting for transfers between devices, shift(): return lax.ppermute(a, axis, [(i, (i + step) % size) for i in range(size)])  27.5 us
    pallas_call x2, Pallas kernels, attend(): pl.pallas_call(functools.partial(attend_kernel, j), out_shape=(half, half...  22.1 us
    all_gather x1, waiting for transfers between devices, on_device(): g1 = lax.all_gather(a1, 'x', axis=0, tiled=False)  20.3 us
    pallas_call x2, Pallas kernels, project(): pl.pallas_call(functools.partial(project_kernel, split), out_shape=[jax.S...  17.2 us
    ppermute x18, starting transfers between devices, shift(): return lax.ppermute(a, axis, [(i, (i + step) % size) for i in range(size)])  16.4 us
    all_to_all x1, blocking collectives, on_device(): out = lax.all_to_all(total, 'x', 0, 0, tiled=True)  10.6 us
    ppermute x4, waiting for transfers between devices, across(): return lax.ppermute(part, ('x', 'zl', 'c'), pairs)  9.14 us
    all_to_all x2, waiting for transfers between devices, over_y(): return add_up(lax.all_to_all(a, 'y', 0, 0, tiled=True))  8.9 us
  transfers between devices with their start and end apart: 27, of which 13 were waited for; matrix products, arithmetic and copies ran while one was open for 8% of the time, Pallas kernels for 23%

profile of v1, /device:TPU:0, one launch (start us, length us, event | category | flops | bytes accessed | tf_op | source)
XLA Modules:
  0.0 196.6 jit_solution(11963177987210719445)
XLA Ops:
  7.7 2.9 %collective-permute-start.3 = (bf16[2,576,128]{2,1,0:T(8,128)(2,1)S(1)}, bf16[2,576,128]{2,1,0:T(8,128)(2,1)}, u32[]{:S(2)}, u32[]{:S(2)}) collective-permute-start(bf16[2,576,128]{2,1,0:T(8,128)(2,1)S(1)} %pad_maximum_fusion.4), channel_id=1, source_target_pairs={{0,96},{1,112},{16,97},{17,113},{32,0},{33,16},{48,1},{49,17},{64,... | collective-permute-start | bytes 884744 | tf_op jit(solution)/shard_map/ppermute | solution.py:258
  13.1 2.6 %constant_dynamic-slice_fusion.1 = (bf16[512,384]{1,0:T(8,128)(2,1)}, bf16[512,384]{1,0:T(8,128)(2,1)}, bf16[512,384]{1,0:T(8,128)(2,1)}, bf16[512,384]{1,0:T(8,128)(2,1)}) fusion(bf16[512,1536]{1,0:T(8,128)(2,1)} %param.6, s32[]{:T(128)S(6)} %select_n.64, s32[]{:T(128)S(6)} %select_n.60, s32[]{:T(128)S(6)} %select_n.58, s32[]{:T(128)S(6)} %select_n.62), kind=kLoop, calls=%fused_computation.16 | loop fusion | bytes 3145744 | tf_op jit(solution)/shard_map/dynamic_slice | solution.py:267
  16.8 6.7 %collective-permute-done.3 = bf16[2,576,128]{2,1,0:T(8,128)(2,1)} collective-permute-done((bf16[2,576,128]{2,1,0:T(8,128)(2,1)S(1)}, bf16[2,576,128]{2,1,0:T(8,128)(2,1)}, u32[]{:S(2)}, u32[]{:S(2)}) %collective-permute-start.3) | collective-permute-done | bytes 294944 | tf_op jit(solution)/shard_map/ppermute | solution.py:258
  25.6 2.4 %collective-permute-done.1 = bf16[2,576,128]{2,1,0:T(8,128)(2,1)S(1)} collective-permute-done((bf16[2,576,128]{2,1,0:T(8,128)(2,1)S(1)}, bf16[2,576,128]{2,1,0:T(8,128)(2,1)S(1)}, u32[]{:S(2)}, u32[]{:S(2)}) %collective-permute-start.1) | collective-permute-done | bytes 294944 | tf_op jit(solution)/shard_map/ppermute | solution.py:258
  28.5 3.0 %collective-permute-start.7 = (bf16[512,384]{1,0:T(8,128)(2,1)S(1)}, bf16[512,384]{1,0:T(8,128)(2,1)S(1)}, u32[]{:S(2)}, u32[]{:S(2)}) collective-permute-start(bf16[512,384]{1,0:T(8,128)(2,1)S(1)} %copy-done.14), channel_id=1, source_target_pairs={{0,64},{32,96},{64,0},{96,32},{1,65},{33,97},{65,1},{97,33},{2,66}... | collective-permute-start | bytes 1179656 | tf_op jit(solution)/shard_map/ppermute | solution.py:27
  35.4 6.4 %collective-permute-done.6.q1 = bf16[512,384]{1,0:T(8,128)(2,1)S(1)} collective-permute-done((bf16[512,384]{1,0:T(8,128)(2,1)S(1)}, bf16[512,384]{1,0:T(8,128)(2,1)S(1)}, u32[]{:S(2)}, u32[]{:S(2)}) %collective-permute-start.6) | collective-permute-done | bytes 393248 | tf_op jit(solution)/shard_map/ppermute | solution.py:27
  42.6 6.5 %collective-permute-done.7.q2 = bf16[512,384]{1,0:T(8,128)(2,1)S(1)} collective-permute-done((bf16[512,384]{1,0:T(8,128)(2,1)S(1)}, bf16[512,384]{1,0:T(8,128)(2,1)S(1)}, u32[]{:S(2)}, u32[]{:S(2)}) %collective-permute-start.7) | collective-permute-done | bytes 393248 | tf_op jit(solution)/shard_map/ppermute | solution.py:27
  53.3 3.4 %keys_values_0.1 = (bf16[2,256,4096]{2,1,0:T(8,128)(2,1)S(1)}, bf16[2,128,4096]{2,1,0:T(8,128)(2,1)S(1)}) custom-call(s32[5]{0:T(128)S(1)} %stack.43.info, s32[16]{0:T(128)S(1)} %copy-done.9, bf16[4,576,128]{2,1,0:T(8,128)(2,1)S(1)} %get-tuple-element.46.refs_0_, bf16[4,576,128]{2,1,0:T(8,128)(2,1)S(1)} %get-tuple-element.59.refs_1_, ...), custom_call_target="tpu_custom_call" | custom-call | flops 3000000000 | bytes 5000000 | tf_op jit(solution)/shard_map/keys_values_0/pallas_call | solution.py:68
  56.8 3.5 %keys_values_1.1 = (bf16[2,256,4096]{2,1,0:T(8,128)(2,1)S(1)}, bf16[2,128,4096]{2,1,0:T(8,128)(2,1)S(1)}) custom-call(s32[5]{0:T(128)S(1)} %stack.43.info, s32[16]{0:T(128)S(1)} %copy-done.9, bf16[4,576,128]{2,1,0:T(8,128)(2,1)} %collective-permute-done.4.refs_0_, ...), custom_call_target="tpu_custom_call", output_to_operand_aliasing={{0}: (8, {}), {1}: (9, {})} | custom-call | flops 3000000000 | bytes 5000000 | tf_op jit(solution)/shard_map/keys_values_1/pallas_call | solution.py:68
  60.4 11.0 %attend_0.1 = (bf16[512,256]{1,0:T(8,128)(2,1)S(1)}, bf16[512,256]{1,0:T(8,128)(2,1)S(1)}) custom-call(s32[5]{0:T(128)S(1)} %stack.43.info, s32[16]{0:T(128)S(1)} %copy-done.9, bf16[512,384]{1,0:T(8,128)(2,1)S(1)} %copy-done.3, bf16[512,384]{1,0:T(8,128)(2,1)S(1)} %copy-done.6, bf16[512,384]{1,0:T(8,128)(2,1)S(1)} %copy-done.8, ...), custom_call_target="tpu_custom_call" | custom-call | flops 10000000000 | bytes 7000000 | tf_op jit(solution)/shard_map/attend_0/pallas_call | solution.py:170
  74.2 2.5 %collective-permute-start.15 = (bf16[512,512]{1,0:T(8,128)(2,1)}, bf16[512,512]{1,0:T(8,128)(2,1)}, u32[]{:S(2)}, u32[]{:S(2)}) collective-permute-start(bf16[512,512]{1,0:T(8,128)(2,1)} %pad_maximum_fusion.2.refs_0_), channel_id=1, source_target_pairs={{0,64},{32,96},{64,0},{96,32},{1,65},{33,97},{65,1},{97,33},{2,66}... | collective-permute-start | bytes 1572872 | tf_op jit(solution)/shard_map/ppermute | solution.py:27
  81.2 11.1 %attend_2.1 = (bf16[512,256]{1,0:T(8,128)(2,1)S(1)}, bf16[512,256]{1,0:T(8,128)(2,1)S(1)}) custom-call(s32[5]{0:T(128)S(1)} %stack.43.info, s32[16]{0:T(128)S(1)} %copy-done.9, bf16[512,384]{1,0:T(8,128)(2,1)S(1)} %copy-done.3, bf16[512,384]{1,0:T(8,128)(2,1)S(1)} %copy-done.6, bf16[512,384]{1,0:T(8,128)(2,1)S(1)} %copy-done.8, ...), custom_call_target="tpu_custom_call" | custom-call | flops 10000000000 | bytes 7000000 | tf_op jit(solution)/shard_map/attend_2/pallas_call | solution.py:170
  94.8 6.1 %collective-permute-done.14.refs_1_ = bf16[512,512]{1,0:T(8,128)(2,1)} collective-permute-done((bf16[512,512]{1,0:T(8,128)(2,1)}, bf16[512,512]{1,0:T(8,128)(2,1)}, u32[]{:S(2)}, u32[]{:S(2)}) %collective-permute-start.14) | collective-permute-done | bytes 524320 | tf_op jit(solution)/shard_map/ppermute | solution.py:27
  101.6 8.3 %project_0.1 = bf16[4,128,1792]{2,1,0:T(8,128)(2,1)} custom-call(s32[5]{0:T(128)} %copy-done.4, bf16[512,512]{1,0:T(8,128)(2,1)} %pad_maximum_fusion.2.refs_0_, bf16[512,512]{1,0:T(8,128)(2,1)} %collective-permute-done.14.refs_1_, bf16[512,512]{1,0:T(8,128)(2,1)} %collective-permute-done.15.refs_2_, bf16[512,512]{1,0:T(8,128)(2,1)} %collective-permute-done.16.refs_3_, ...), custom_call_target="tpu_custom_call" | custom-call | flops 4000000000 | bytes 7000000 | tf_op jit(solution)/shard_map/project_0/pallas_call | solution.py:228
  109.9 4.5 %all-to-all-start = ((bf16[4,128,1792]{2,1,0:T(8,128)(2,1)}), bf16[4,128,1792]{2,1,0:T(8,128)(2,1)}, u32[]{:S(2)}, u32[]{:S(2)}) async-start(bf16[4,128,1792]{2,1,0:T(8,128)(2,1)} %project_0.1), calls=%async_computation | async-start | bytes 3670016 | tf_op jit(solution)/shard_map/all_to_all | solution.py:305
  114.4 20.3 %all-gather.6.cloned.1.call-done = bf16[2048,512]{1,0:T(8,128)(2,1)} async-done(((bf16[512,512]{1,0:T(8,128)(2,1)}), bf16[2048,512]{1,0:T(8,128)(2,1)}) %all-gather.6.cloned.1.call-update) | async-done | bytes 2097168 | tf_op jit(solution)/shard_map/all_gather | solution.py:291
  134.7 8.8 %project_1.1 = (bf16[4,128,896]{2,1,0:T(8,128)(2,1)}, bf16[4,64,896]{2,1,0:T(8,128)(2,1)}, bf16[4,64,896]{2,1,0:T(8,128)(2,1)}) custom-call(s32[5]{0:T(128)} %copy-done.4, bf16[4,512,512]{2,1,0:T(8,128)(2,1)} %bitcast.41, bf16[1024,1792]{1,0:T(8,128)(2,1)} %all-gather.4.cloned.1.call-done.refs_4_.refs_1_, ...), custom_call_target="tpu_custom_call" | custom-call | flops 4000000000 | bytes 7000000 | tf_op jit(solution)/shard_map/project_1/pallas_call | solution.py:228
  143.5 3.2 %collective-permute-start.21 = (bf16[4,64,896]{2,1,0:T(8,128)(2,1)}, bf16[4,64,896]{2,1,0:T(8,128)(2,1)}, u32[]{:S(2)}, u32[]{:S(2)}) collective-permute-start(bf16[4,64,896]{2,1,0:T(8,128)(2,1)} %get-tuple-element.86), channel_id=1, source_target_pairs={{0,8},{8,0},{1,9},{9,1},{2,10},{10,2},{3,11},{11,3},{4,12},{12,4},... | collective-permute-start | bytes 1376264 | tf_op jit(solution)/shard_map/ppermute | solution.py:27
  146.7 4.3 %all-to-all-start.1 = ((bf16[4,128,896]{2,1,0:T(8,128)(2,1)}), bf16[4,128,896]{2,1,0:T(8,128)(2,1)S(1)}, u32[]{:S(2)}, u32[]{:S(2)}) async-start(bf16[4,128,896]{2,1,0:T(8,128)(2,1)} %get-tuple-element.84), calls=%async_computation.1 | async-start | bytes 1835008 | tf_op jit(solution)/shard_map/all_to_all | solution.py:294
  153.9 4.1 %collective-permute-done.21 = bf16[4,64,896]{2,1,0:T(8,128)(2,1)} collective-permute-done((bf16[4,64,896]{2,1,0:T(8,128)(2,1)}, bf16[4,64,896]{2,1,0:T(8,128)(2,1)}, u32[]{:S(2)}, u32[]{:S(2)}) %collective-permute-start.21) | collective-permute-done | bytes 458784 | tf_op jit(solution)/shard_map/ppermute | solution.py:27
  160.0 4.4 %all-to-all-done.1 = bf16[4,128,896]{2,1,0:T(8,128)(2,1)S(1)} async-done(((bf16[4,128,896]{2,1,0:T(8,128)(2,1)}), bf16[4,128,896]{2,1,0:T(8,128)(2,1)S(1)}, u32[]{:S(2)}, u32[]{:S(2)}) %all-to-all-start.1) | async-done | bytes 917536 | tf_op jit(solution)/shard_map/all_to_all | solution.py:294
  164.4 4.1 %all-to-all-start.2 = ((bf16[4,64,896]{2,1,0:T(8,128)(2,1)}), bf16[4,64,896]{2,1,0:T(8,128)(2,1)}, u32[]{:S(2)}, u32[]{:S(2)}) async-start(bf16[4,64,896]{2,1,0:T(8,128)(2,1)} %add_convert_fusion), calls=%async_computation.2 | async-start | bytes 917504 | tf_op jit(solution)/shard_map/all_to_all | solution.py:294
  171.8 4.5 %all-to-all-done.2 = bf16[4,64,896]{2,1,0:T(8,128)(2,1)} async-done(((bf16[4,64,896]{2,1,0:T(8,128)(2,1)}), bf16[4,64,896]{2,1,0:T(8,128)(2,1)}, u32[]{:S(2)}, u32[]{:S(2)}) %all-to-all-start.2) | async-done | bytes 458784 | tf_op jit(solution)/shard_map/all_to_all | solution.py:294
  178.4 10.6 %all_to_all.20 = bf16[4,32,1792]{2,1,0:T(8,128)(2,1)S(1)} all-to-all(bf16[4,32,1792]{2,1,0:T(8,128)(2,1)S(1)} %maximum_maximum_fusion), channel_id=1, replica_groups=mesh['x'=4,'zl'=2,'zh'=2,'y'=4,'c'=2] {'x'}, dimensions={0} | all-to-all | bytes 917504 | tf_op jit(solution)/shard_map/all_to_all | solution.py:312
  (97 shorter events, 37.5 us)
Async XLA Ops:
  6.5 67.3 %all-gather.4.cloned.1.call-start = ((), (), s32[]{:S(2)}) async-start(), calls=%async_computation.4 | async-start | bytes 5505024 | tf_op jit(solution)/shard_map/all_gather | solution.py:248
  7.7 15.7 %collective-permute-start.3 = (bf16[2,576,128]{2,1,0:T(8,128)(2,1)S(1)}, bf16[2,576,128]{2,1,0:T(8,128)(2,1)}, u32[]{:S(2)}, u32[]{:S(2)}) collective-permute-start(bf16[2,576,128]{2,1,0:T(8,128)(2,1)S(1)} %pad_maximum_fusion.4), channel_id=1, source_target_pairs={{0,96},{1,112},{16,97},{17,113},{32,0},{33,16},{48,1},{49,17},{64,... | collective-permute-start | bytes 884744 | tf_op jit(solution)/shard_map/ppermute | solution.py:258
  10.6 13.9 %collective-permute-start.2 = (bf16[2,576,128]{2,1,0:T(8,128)(2,1)S(1)}, bf16[2,576,128]{2,1,0:T(8,128)(2,1)}, u32[]{:S(2)}, u32[]{:S(2)}) collective-permute-start(bf16[2,576,128]{2,1,0:T(8,128)(2,1)S(1)} %pad_maximum_fusion.4), channel_id=1, source_target_pairs={{0,64},{1,80},{16,65},{17,81},{32,96},{33,112},{48,97},{49,113},{6... | collective-permute-start | bytes 884744 | tf_op jit(solution)/shard_map/ppermute | solution.py:258
  11.4 16.6 %collective-permute-start.1 = (bf16[2,576,128]{2,1,0:T(8,128)(2,1)S(1)}, bf16[2,576,128]{2,1,0:T(8,128)(2,1)S(1)}, u32[]{:S(2)}, u32[]{:S(2)}) collective-permute-start(bf16[2,576,128]{2,1,0:T(8,128)(2,1)S(1)} %pad_maximum_fusion.4), channel_id=1, source_target_pairs={{0,32},{1,48},{16,33},{17,49},{32,64},{33,80},{48,65},{49,81},{64,... | collective-permute-start | bytes 884744 | tf_op jit(solution)/shard_map/ppermute | solution.py:258
  12.3 15.7 %collective-permute-start = (bf16[2,576,128]{2,1,0:T(8,128)(2,1)S(1)}, bf16[2,576,128]{2,1,0:T(8,128)(2,1)S(1)}, u32[]{:S(2)}, u32[]{:S(2)}) collective-permute-start(bf16[2,576,128]{2,1,0:T(8,128)(2,1)S(1)} %pad_maximum_fusion.4), channel_id=1, source_target_pairs={{0,0},{1,16},{16,1},{17,17},{32,32},{33,48},{48,33},{49,49},{64,64... | collective-permute-start | bytes 884744 | tf_op jit(solution)/shard_map/ppermute | solution.py:258
  13.0 121.7 %all-gather.6.cloned.1.call-start = ((), (), s32[]{:S(2)}) async-start(), calls=%async_computation.5 | async-start | bytes 2621440 | tf_op jit(solution)/shard_map/all_gather | solution.py:291
  28.4 13.4 %collective-permute-start.6 = (bf16[512,384]{1,0:T(8,128)(2,1)S(1)}, bf16[512,384]{1,0:T(8,128)(2,1)S(1)}, u32[]{:S(2)}, u32[]{:S(2)}) collective-permute-start(bf16[512,384]{1,0:T(8,128)(2,1)S(1)} %copy-done.15), channel_id=1, source_target_pairs={{0,32},{32,64},{64,96},{96,0},{1,33},{33,65},{65,97},{97,1},{2,34}... | collective-permute-start | bytes 1179656 | tf_op jit(solution)/shard_map/ppermute | solution.py:27
  28.5 20.6 %collective-permute-start.7 = (bf16[512,384]{1,0:T(8,128)(2,1)S(1)}, bf16[512,384]{1,0:T(8,128)(2,1)S(1)}, u32[]{:S(2)}, u32[]{:S(2)}) collective-permute-start(bf16[512,384]{1,0:T(8,128)(2,1)S(1)} %copy-done.14), channel_id=1, source_target_pairs={{0,64},{32,96},{64,0},{96,32},{1,65},{33,97},{65,1},{97,33},{2,66}... | collective-permute-start | bytes 1179656 | tf_op jit(solution)/shard_map/ppermute | solution.py:27
  31.5 19.1 %collective-permute-start.4 = (bf16[4,576,128]{2,1,0:T(8,128)(2,1)S(1)}, bf16[4,576,128]{2,1,0:T(8,128)(2,1)}, u32[]{:S(2)}, u32[]{:S(2)}) collective-permute-start(bf16[4,576,128]{2,1,0:T(8,128)(2,1)S(1)} %get-tuple-element.46.refs_0_), channel_id=1, source_target_pairs={{0,2},{2,4},{4,6},{6,0},{1,3},{3,5},{5,7},{7,1},{8,10},{10,12},{12... | collective-permute-start | bytes 1769480 | tf_op jit(solution)/shard_map/ppermute | solution.py:27
  33.1 17.5 %collective-permute-start.5 = (bf16[4,576,128]{2,1,0:T(8,128)(2,1)S(1)}, bf16[4,576,128]{2,1,0:T(8,128)(2,1)}, u32[]{:S(2)}, u32[]{:S(2)}) collective-permute-start(bf16[4,576,128]{2,1,0:T(8,128)(2,1)S(1)} %get-tuple-element.46.refs_0_), channel_id=1, source_target_pairs={{0,6},{2,0},{4,2},{6,4},{1,7},{3,1},{5,3},{7,5},{8,14},{10,8},{12,... | collective-permute-start | bytes 1769480 | tf_op jit(solution)/shard_map/ppermute | solution.py:27
  34.8 15.8 %collective-permute-start.8 = (bf16[512,384]{1,0:T(8,128)(2,1)}, bf16[512,384]{1,0:T(8,128)(2,1)}, u32[]{:S(2)}, u32[]{:S(2)}) collective-permute-start(bf16[512,384]{1,0:T(8,128)(2,1)} %get-tuple-element.49), channel_id=1, source_target_pairs={{0,96},{32,0},{64,32},{96,64},{1,97},{33,1},{65,33},{97,65},{2,98}... | collective-permute-start | bytes 1179656 | tf_op jit(solution)/shard_map/ppermute | solution.py:27
  42.6 8.6 %collective-permute-start.11 = (bf16[4,576,128]{2,1,0:T(8,128)(2,1)S(1)}, bf16[4,576,128]{2,1,0:T(8,128)(2,1)}, u32[]{:S(2)}, u32[]{:S(2)}) collective-permute-start(bf16[4,576,128]{2,1,0:T(8,128)(2,1)S(1)} %get-tuple-element.46.refs_0_), channel_id=1, source_target_pairs={{0,1},{1,0},{2,3},{3,2},{4,5},{5,4},{6,7},{7,6},{8,9},{9,8},{10,11... | collective-permute-start | bytes 1769480 | tf_op jit(solution)/shard_map/ppermute | solution.py:27
  50.6 6.2 %collective-permute-start.9 = (bf16[4,576,128]{2,1,0:T(8,128)(2,1)}, bf16[4,576,128]{2,1,0:T(8,128)(2,1)S(1)}, u32[]{:S(2)}, u32[]{:S(2)}) collective-permute-start(bf16[4,576,128]{2,1,0:T(8,128)(2,1)} %collective-permute-done.4.refs_0_), channel_id=1, source_target_pairs={{0,1},{1,0},{2,3},{3,2},{4,5},{5,4},{6,7},{7,6},{8,9},{9,8},{10,11... | collective-permute-start | bytes 1769480 | tf_op jit(solution)/shard_map/ppermute | solution.py:27
  50.7 6.1 %collective-permute-start.10 = (bf16[4,576,128]{2,1,0:T(8,128)(2,1)}, bf16[4,576,128]{2,1,0:T(8,128)(2,1)S(1)}, u32[]{:S(2)}, u32[]{:S(2)}) collective-permute-start(bf16[4,576,128]{2,1,0:T(8,128)(2,1)} %collective-permute-done.5.refs_1_), channel_id=1, source_target_pairs={{0,1},{1,0},{2,3},{3,2},{4,5},{5,4},{6,7},{7,6},{8,9},{9,8},{10,11... | collective-permute-start | bytes 1769480 | tf_op jit(solution)/shard_map/ppermute | solution.py:27
  73.8 27.7 %collective-permute-start.18 = (bf16[1024,1792]{1,0:T(8,128)(2,1)}, bf16[1024,1792]{1,0:T(8,128)(2,1)}, u32[]{:S(2)}, u32[]{:S(2)}) collective-permute-start(bf16[1024,1792]{1,0:T(8,128)(2,1)} %all-gather.4.cloned.1.call-done.refs_4_.refs_1_), channel_id=1, source_target_pairs={{0,1},{1,0},{2,3},{3,2},{4,5},{5,4},{6,7},{7,6},{8,9},{9,8},{10,11... | collective-permute-start | bytes 11010056 | tf_op jit(solution)/shard_map/ppermute | solution.py:27
  74.2 26.7 %collective-permute-start.14 = (bf16[512,512]{1,0:T(8,128)(2,1)}, bf16[512,512]{1,0:T(8,128)(2,1)}, u32[]{:S(2)}, u32[]{:S(2)}) collective-permute-start(bf16[512,512]{1,0:T(8,128)(2,1)} %pad_maximum_fusion.2.refs_0_), channel_id=1, source_target_pairs={{0,32},{32,64},{64,96},{96,0},{1,33},{33,65},{65,97},{97,1},{2,34}... | collective-permute-start | bytes 1572872 | tf_op jit(solution)/shard_map/ppermute | solution.py:27
  74.2 26.7 %collective-permute-start.15 = (bf16[512,512]{1,0:T(8,128)(2,1)}, bf16[512,512]{1,0:T(8,128)(2,1)}, u32[]{:S(2)}, u32[]{:S(2)}) collective-permute-start(bf16[512,512]{1,0:T(8,128)(2,1)} %pad_maximum_fusion.2.refs_0_), channel_id=1, source_target_pairs={{0,64},{32,96},{64,0},{96,32},{1,65},{33,97},{65,1},{97,33},{2,66}... | collective-permute-start | bytes 1572872 | tf_op jit(solution)/shard_map/ppermute | solution.py:27
  76.8 24.8 %collective-permute-start.16 = (bf16[512,512]{1,0:T(8,128)(2,1)}, bf16[512,512]{1,0:T(8,128)(2,1)}, u32[]{:S(2)}, u32[]{:S(2)}) collective-permute-start(bf16[512,512]{1,0:T(8,128)(2,1)} %pad_maximum_fusion.2.refs_0_), channel_id=1, source_target_pairs={{0,96},{32,0},{64,32},{96,64},{1,97},{33,1},{65,33},{97,65},{2,98}... | collective-permute-start | bytes 1572872 | tf_op jit(solution)/shard_map/ppermute | solution.py:27
  109.9 33.6 %all-to-all-start = ((bf16[4,128,1792]{2,1,0:T(8,128)(2,1)}), bf16[4,128,1792]{2,1,0:T(8,128)(2,1)}, u32[]{:S(2)}, u32[]{:S(2)}) async-start(bf16[4,128,1792]{2,1,0:T(8,128)(2,1)} %project_0.1), calls=%async_computation | async-start | bytes 3670016 | tf_op jit(solution)/shard_map/all_to_all | solution.py:305
  143.5 14.4 %collective-permute-start.21 = (bf16[4,64,896]{2,1,0:T(8,128)(2,1)}, bf16[4,64,896]{2,1,0:T(8,128)(2,1)}, u32[]{:S(2)}, u32[]{:S(2)}) collective-permute-start(bf16[4,64,896]{2,1,0:T(8,128)(2,1)} %get-tuple-element.86), channel_id=1, source_target_pairs={{0,8},{8,0},{1,9},{9,1},{2,10},{10,2},{3,11},{11,3},{4,12},{12,4},... | collective-permute-start | bytes 1376264 | tf_op jit(solution)/shard_map/ppermute | solution.py:27
  146.7 17.7 %all-to-all-start.1 = ((bf16[4,128,896]{2,1,0:T(8,128)(2,1)}), bf16[4,128,896]{2,1,0:T(8,128)(2,1)S(1)}, u32[]{:S(2)}, u32[]{:S(2)}) async-start(bf16[4,128,896]{2,1,0:T(8,128)(2,1)} %get-tuple-element.84), calls=%async_computation.1 | async-start | bytes 1835008 | tf_op jit(solution)/shard_map/all_to_all | solution.py:294
  153.5 17.3 %collective-permute-start.19 = (bf16[2,32,1792]{2,1,0:T(8,128)(2,1)}, bf16[2,32,1792]{2,1,0:T(8,128)(2,1)}, u32[]{:S(2)}, u32[]{:S(2)}) collective-permute-start(bf16[2,32,1792]{2,1,0:T(8,128)(2,1)} %dynamic-slice_bitcast_fusion), channel_id=1, source_target_pairs={{0,8},{8,0},{1,9},{9,1},{2,10},{10,2},{3,11},{11,3},{4,12},{12,4},... | collective-permute-start | bytes 688136 | tf_op jit(solution)/shard_map/ppermute | solution.py:27
  164.4 11.9 %all-to-all-start.2 = ((bf16[4,64,896]{2,1,0:T(8,128)(2,1)}), bf16[4,64,896]{2,1,0:T(8,128)(2,1)}, u32[]{:S(2)}, u32[]{:S(2)}) async-start(bf16[4,64,896]{2,1,0:T(8,128)(2,1)} %add_convert_fusion), calls=%async_computation.2 | async-start | bytes 917504 | tf_op jit(solution)/shard_map/all_to_all | solution.py:294
  170.3 7.1 %collective-permute-start.20 = (bf16[2,32,896]{2,1,0:T(8,128)(2,1)S(1)}, bf16[2,32,896]{2,1,0:T(8,128)(2,1)S(1)}, u32[]{:S(2)}, u32[]{:S(2)}) collective-permute-start(bf16[2,32,896]{2,1,0:T(8,128)(2,1)S(1)} %dynamic-slice_bitcast_fusion.3), channel_id=1, source_target_pairs={{0,8},{8,0},{1,9},{9,1},{2,10},{10,2},{3,11},{11,3},{4,12},{12,4},... | collective-permute-start | bytes 344072 | tf_op jit(solution)/shard_map/ppermute | solution.py:27
  (20 other events, 123.6 us)
Sparse Core Ops, SparseCore 0:
  13.2 58.1 all-gather.3
  101.7 32.9 all-gather.5

commit v2 on v1

--- a/solution.py
+++ b/solution.py
@@ -232,7 +232,7 @@
         in_specs=[SMEM] + whole + [column, column],
         out_specs=out_specs,
         compiler_params=params(56),
-        cost_estimate=cost(4 * 10**9, 7 * 10**6),
+        cost_estimate=cost(4 * 10**9 if split else 4 * 10**10, 7 * 10**6),
         name=f"project_{j}",
     )(info, *ctx, w, w_far)
 
@@ -287,8 +287,8 @@
     a0, info2, w = hold(attention(0, info1), info1, w)
     w_far = shift(w, "c", 2, 1)
     g0, a1 = [a0] + [shift(a0, "x", NX, s) for s in (1, 2, 3)], attention(2, info2)
+    g1 = lax.all_gather(a1, "x", axis=0, tiled=False)
     g0, a1, info3, w_far = hold(g0, a1, info2, w_far)
-    g1 = lax.all_gather(a1, "x", axis=0, tiled=False)
 
     def over_y(a):
         return add_up(lax.all_to_all(a, "y", 0, 0, tiled=True))

time: 197 us -> 192 us (0.975)
  waiting for transfers between devices: 65.9 us -> 59 us
  Pallas kernels: 46.2 us -> 43.4 us
    all_gather x1, waiting for transfers between devices: 20.3 us -> 13.4 us  [on_device(): g1 = lax.all_gather(a1, 'x', axis=0, tiled=False)]
    all_to_all x2, waiting for transfers between devices: 8.9 us -> 6.07 us  [over_y(): return add_up(lax.all_to_all(a, 'y', 0, 0, tiled=True))]
    pallas_call x2, Pallas kernels: 22.1 us -> 19.4 us  [attend(): pl.pallas_call(functools.partial(attend_kernel, j), out_shape=(half, half...]
    ppermute x18, starting transfers between devices: 16.4 us -> 19.1 us  [shift(): return lax.ppermute(a, axis, [(i, (i + step) % size) for i in range(size)])]
    ppermute x18, waiting for transfers between devices: 27.5 us -> 29.6 us  [shift(): return lax.ppermute(a, axis, [(i, (i + step) % size) for i in range(size)])]
    unnamed x35 -> x38, local copies, waits for them, and re-layouts: 7.39 us -> 8.17 us
  transfers between devices with their start and end apart: 27 -> 27, of which waited for: 13 -> 14; matrix products, arithmetic and copies ran while one was open for 8% -> 8% of each run, Pallas kernels for 23% -> 23%
where the time goes in v2:
time: 192 us; the launch traced here: 190 us
  waiting for transfers between devices  59 us (31%)
  Pallas kernels  43.4 us (23%)
  starting transfers between devices  36.5 us (19%)
  local copies, waits for them, and re-layouts  16.7 us (9%)
  between operations  13.9 us (7%)
  blocking collectives  12.2 us (6%)
  other arithmetic  8.82 us (5%)
    ppermute x18, waiting for transfers between devices, shift(): return lax.ppermute(a, axis, [(i, (i + step) % size) for i in range(size)])  29.6 us
    pallas_call x2, Pallas kernels, attend(): pl.pallas_call(functools.partial(attend_kernel, j), out_shape=(half, half...  19.4 us
    ppermute x18, starting transfers between devices, shift(): return lax.ppermute(a, axis, [(i, (i + step) % size) for i in range(size)])  19.1 us
    pallas_call x2, Pallas kernels, project(): pl.pallas_call(functools.partial(project_kernel, split), out_shape=[jax.S...  17.1 us
    all_gather x1, waiting for transfers between devices, on_device(): g1 = lax.all_gather(a1, 'x', axis=0, tiled=False)  13.4 us
    all_to_all x1, blocking collectives, on_device(): out = lax.all_to_all(total, 'x', 0, 0, tiled=True)  12.2 us
    ppermute x4, waiting for transfers between devices, across(): return lax.ppermute(part, ('x', 'zl', 'c'), pairs)  9.15 us
    unnamed x38, local copies, waits for them, and re-layouts  8.17 us
  transfers between devices with their start and end apart: 27, of which 14 were waited for; matrix products, arithmetic and copies ran while one was open for 8% of the time, Pallas kernels for 23%

profile of v2, /device:TPU:0, one launch (start us, length us, event | category | flops | bytes accessed | tf_op | source)
XLA Modules:
  0.0 190.4 jit_solution(11908636440095057729)
XLA Ops:
  7.7 2.9 %collective-permute-start.3 = (bf16[2,576,128]{2,1,0:T(8,128)(2,1)S(1)}, bf16[2,576,128]{2,1,0:T(8,128)(2,1)}, u32[]{:S(2)}, u32[]{:S(2)}) collective-permute-start(bf16[2,576,128]{2,1,0:T(8,128)(2,1)S(1)} %pad_maximum_fusion.3), channel_id=1, source_target_pairs={{0,96},{1,112},{16,97},{17,113},{32,0},{33,16},{48,1},{49,17},{64,... | collective-permute-start | bytes 884744 | tf_op jit(solution)/shard_map/ppermute | solution.py:258
  13.1 2.6 %constant_dynamic-slice_fusion.1 = (bf16[512,384]{1,0:T(8,128)(2,1)}, bf16[512,384]{1,0:T(8,128)(2,1)}, bf16[512,384]{1,0:T(8,128)(2,1)}, bf16[512,384]{1,0:T(8,128)(2,1)}) fusion(bf16[512,1536]{1,0:T(8,128)(2,1)} %param.6, s32[]{:T(128)S(6)} %select_n.64, s32[]{:T(128)S(6)} %select_n.60, s32[]{:T(128)S(6)} %select_n.58, s32[]{:T(128)S(6)} %select_n.62), kind=kLoop, calls=%fused_computation.17 | loop fusion | bytes 3145744 | tf_op jit(solution)/shard_map/dynamic_slice | solution.py:267
  16.7 6.7 %collective-permute-done.3 = bf16[2,576,128]{2,1,0:T(8,128)(2,1)} collective-permute-done((bf16[2,576,128]{2,1,0:T(8,128)(2,1)S(1)}, bf16[2,576,128]{2,1,0:T(8,128)(2,1)}, u32[]{:S(2)}, u32[]{:S(2)}) %collective-permute-start.3) | collective-permute-done | bytes 294944 | tf_op jit(solution)/shard_map/ppermute | solution.py:258
  25.6 2.4 %collective-permute-done.1 = bf16[2,576,128]{2,1,0:T(8,128)(2,1)S(1)} collective-permute-done((bf16[2,576,128]{2,1,0:T(8,128)(2,1)S(1)}, bf16[2,576,128]{2,1,0:T(8,128)(2,1)S(1)}, u32[]{:S(2)}, u32[]{:S(2)}) %collective-permute-start.1) | collective-permute-done | bytes 294944 | tf_op jit(solution)/shard_map/ppermute | solution.py:258
  28.5 3.0 %collective-permute-start.7 = (bf16[512,384]{1,0:T(8,128)(2,1)S(1)}, bf16[512,384]{1,0:T(8,128)(2,1)S(1)}, u32[]{:S(2)}, u32[]{:S(2)}) collective-permute-start(bf16[512,384]{1,0:T(8,128)(2,1)S(1)} %copy-done.15), channel_id=1, source_target_pairs={{0,64},{32,96},{64,0},{96,32},{1,65},{33,97},{65,1},{97,33},{2,66}... | collective-permute-start | bytes 1179656 | tf_op jit(solution)/shard_map/ppermute | solution.py:27
  35.4 6.4 %collective-permute-done.6.q1 = bf16[512,384]{1,0:T(8,128)(2,1)S(1)} collective-permute-done((bf16[512,384]{1,0:T(8,128)(2,1)S(1)}, bf16[512,384]{1,0:T(8,128)(2,1)S(1)}, u32[]{:S(2)}, u32[]{:S(2)}) %collective-permute-start.6) | collective-permute-done | bytes 393248 | tf_op jit(solution)/shard_map/ppermute | solution.py:27
  42.5 6.5 %collective-permute-done.7.q2 = bf16[512,384]{1,0:T(8,128)(2,1)S(1)} collective-permute-done((bf16[512,384]{1,0:T(8,128)(2,1)S(1)}, bf16[512,384]{1,0:T(8,128)(2,1)S(1)}, u32[]{:S(2)}, u32[]{:S(2)}) %collective-permute-start.7) | collective-permute-done | bytes 393248 | tf_op jit(solution)/shard_map/ppermute | solution.py:27
  53.3 3.4 %keys_values_0.1 = (bf16[2,256,4096]{2,1,0:T(8,128)(2,1)S(1)}, bf16[2,128,4096]{2,1,0:T(8,128)(2,1)S(1)}) custom-call(s32[5]{0:T(128)S(1)} %stack.43.info, s32[16]{0:T(128)S(1)} %copy-done.9, bf16[4,576,128]{2,1,0:T(8,128)(2,1)S(1)} %get-tuple-element.45.refs_0_, bf16[4,576,128]{2,1,0:T(8,128)(2,1)S(1)} %get-tuple-element.58.refs_1_, ...), custom_call_target="tpu_custom_call" | custom-call | flops 3000000000 | bytes 5000000 | tf_op jit(solution)/shard_map/keys_values_0/pallas_call | solution.py:68
  56.8 3.5 %keys_values_1.1 = (bf16[2,256,4096]{2,1,0:T(8,128)(2,1)S(1)}, bf16[2,128,4096]{2,1,0:T(8,128)(2,1)S(1)}) custom-call(s32[5]{0:T(128)S(1)} %stack.43.info, s32[16]{0:T(128)S(1)} %copy-done.9, bf16[4,576,128]{2,1,0:T(8,128)(2,1)} %collective-permute-done.4.refs_0_, ...), custom_call_target="tpu_custom_call", output_to_operand_aliasing={{0}: (8, {}), {1}: (9, {})} | custom-call | flops 3000000000 | bytes 5000000 | tf_op jit(solution)/shard_map/keys_values_1/pallas_call | solution.py:68
  60.4 10.0 %attend_0.1 = (bf16[512,256]{1,0:T(8,128)(2,1)S(1)}, bf16[512,256]{1,0:T(8,128)(2,1)S(1)}) custom-call(s32[5]{0:T(128)S(1)} %stack.43.info, s32[16]{0:T(128)S(1)} %copy-done.9, bf16[512,384]{1,0:T(8,128)(2,1)S(1)} %copy-done.3, bf16[512,384]{1,0:T(8,128)(2,1)S(1)} %copy-done.6, bf16[512,384]{1,0:T(8,128)(2,1)S(1)} %copy-done.8, ...), custom_call_target="tpu_custom_call" | custom-call | flops 10000000000 | bytes 7000000 | tf_op jit(solution)/shard_map/attend_0/pallas_call | solution.py:170
  73.3 2.6 %collective-permute-start.15 = (bf16[512,512]{1,0:T(8,128)(2,1)}, bf16[512,512]{1,0:T(8,128)(2,1)}, u32[]{:S(2)}, u32[]{:S(2)}) collective-permute-start(bf16[512,512]{1,0:T(8,128)(2,1)} %pad_maximum_fusion.2.refs_0_), channel_id=1, source_target_pairs={{0,64},{32,96},{64,0},{96,32},{1,65},{33,97},{65,1},{97,33},{2,66}... | collective-permute-start | bytes 1572872 | tf_op jit(solution)/shard_map/ppermute | solution.py:27
  80.8 9.4 %attend_2.1 = (bf16[512,256]{1,0:T(8,128)(2,1)S(1)}, bf16[512,256]{1,0:T(8,128)(2,1)S(1)}) custom-call(s32[5]{0:T(128)S(1)} %stack.43.info, s32[16]{0:T(128)S(1)} %copy-done.9, bf16[512,384]{1,0:T(8,128)(2,1)S(1)} %copy-done.3, bf16[512,384]{1,0:T(8,128)(2,1)S(1)} %copy-done.6, bf16[512,384]{1,0:T(8,128)(2,1)S(1)} %copy-done.8, ...), custom_call_target="tpu_custom_call" | custom-call | flops 10000000000 | bytes 7000000 | tf_op jit(solution)/shard_map/attend_2/pallas_call | solution.py:170
  92.6 7.4 %collective-permute-done.14.refs_1_ = bf16[512,512]{1,0:T(8,128)(2,1)} collective-permute-done((bf16[512,512]{1,0:T(8,128)(2,1)}, bf16[512,512]{1,0:T(8,128)(2,1)}, u32[]{:S(2)}, u32[]{:S(2)}) %collective-permute-start.14) | collective-permute-done | bytes 524320 | tf_op jit(solution)/shard_map/ppermute | solution.py:27
  100.6 8.3 %project_0.1 = bf16[4,128,1792]{2,1,0:T(8,128)(2,1)} custom-call(s32[5]{0:T(128)} %copy-done.4, bf16[512,512]{1,0:T(8,128)(2,1)} %pad_maximum_fusion.2.refs_0_, bf16[512,512]{1,0:T(8,128)(2,1)} %collective-permute-done.14.refs_1_, bf16[512,512]{1,0:T(8,128)(2,1)} %collective-permute-done.15.refs_2_, bf16[512,512]{1,0:T(8,128)(2,1)} %collective-permute-done.16.refs_3_, ...), custom_call_target="tpu_custom_call" | custom-call | flops 40000000000 | bytes 7000000 | tf_op jit(solution)/shard_map/project_0/pallas_call | solution.py:228
  108.9 4.4 %all-to-all-start = ((bf16[4,128,1792]{2,1,0:T(8,128)(2,1)}), bf16[4,128,1792]{2,1,0:T(8,128)(2,1)}, u32[]{:S(2)}, u32[]{:S(2)}) async-start(bf16[4,128,1792]{2,1,0:T(8,128)(2,1)} %project_0.1), calls=%async_computation | async-start | bytes 3670016 | tf_op jit(solution)/shard_map/all_to_all | solution.py:305
  113.4 13.4 %all-gather.6.cloned.1.call-done = bf16[2048,512]{1,0:T(8,128)(2,1)} async-done(((bf16[512,512]{1,0:T(8,128)(2,1)}), bf16[2048,512]{1,0:T(8,128)(2,1)}) %all-gather.6.cloned.1.call-update) | async-done | bytes 2097168 | tf_op jit(solution)/shard_map/all_gather | solution.py:290
  126.8 8.8 %project_1.1 = (bf16[4,128,896]{2,1,0:T(8,128)(2,1)}, bf16[4,64,896]{2,1,0:T(8,128)(2,1)}, bf16[4,64,896]{2,1,0:T(8,128)(2,1)}) custom-call(s32[5]{0:T(128)} %copy-done.4, bf16[4,512,512]{2,1,0:T(8,128)(2,1)} %bitcast.41, bf16[1024,1792]{1,0:T(8,128)(2,1)} %all-gather.4.cloned.1.call-done.refs_4_.refs_1_, ...), custom_call_target="tpu_custom_call" | custom-call | flops 4000000000 | bytes 7000000 | tf_op jit(solution)/shard_map/project_1/pallas_call | solution.py:228
  136.3 4.7 %collective-permute-start.21 = (bf16[4,64,896]{2,1,0:T(8,128)(2,1)}, bf16[4,64,896]{2,1,0:T(8,128)(2,1)}, u32[]{:S(2)}, u32[]{:S(2)}) collective-permute-start(bf16[4,64,896]{2,1,0:T(8,128)(2,1)} %get-tuple-element.84), channel_id=1, source_target_pairs={{0,8},{8,0},{1,9},{9,1},{2,10},{10,2},{3,11},{11,3},{4,12},{12,4},... | collective-permute-start | bytes 1376264 | tf_op jit(solution)/shard_map/ppermute | solution.py:27
  141.1 3.5 %all-to-all-start.1 = ((bf16[4,128,896]{2,1,0:T(8,128)(2,1)}), bf16[4,128,896]{2,1,0:T(8,128)(2,1)S(1)}, u32[]{:S(2)}, u32[]{:S(2)}) async-start(bf16[4,128,896]{2,1,0:T(8,128)(2,1)} %get-tuple-element.82), calls=%async_computation.1 | async-start | bytes 1835008 | tf_op jit(solution)/shard_map/all_to_all | solution.py:294
  147.1 4.8 %collective-permute-done.21 = bf16[4,64,896]{2,1,0:T(8,128)(2,1)} collective-permute-done((bf16[4,64,896]{2,1,0:T(8,128)(2,1)}, bf16[4,64,896]{2,1,0:T(8,128)(2,1)}, u32[]{:S(2)}, u32[]{:S(2)}) %collective-permute-start.21) | collective-permute-done | bytes 458784 | tf_op jit(solution)/shard_map/ppermute | solution.py:27
  154.0 2.6 %all-to-all-done.1 = bf16[4,128,896]{2,1,0:T(8,128)(2,1)S(1)} async-done(((bf16[4,128,896]{2,1,0:T(8,128)(2,1)}), bf16[4,128,896]{2,1,0:T(8,128)(2,1)S(1)}, u32[]{:S(2)}, u32[]{:S(2)}) %all-to-all-start.1) | async-done | bytes 917536 | tf_op jit(solution)/shard_map/all_to_all | solution.py:294
  156.6 4.1 %all-to-all-start.2 = ((bf16[4,64,896]{2,1,0:T(8,128)(2,1)}), bf16[4,64,896]{2,1,0:T(8,128)(2,1)}, u32[]{:S(2)}, u32[]{:S(2)}) async-start(bf16[4,64,896]{2,1,0:T(8,128)(2,1)} %add_convert_fusion), calls=%async_computation.2 | async-start | bytes 917504 | tf_op jit(solution)/shard_map/all_to_all | solution.py:294
  165.0 3.5 %all-to-all-done.2 = bf16[4,64,896]{2,1,0:T(8,128)(2,1)} async-done(((bf16[4,64,896]{2,1,0:T(8,128)(2,1)}), bf16[4,64,896]{2,1,0:T(8,128)(2,1)}, u32[]{:S(2)}, u32[]{:S(2)}) %all-to-all-start.2) | async-done | bytes 458784 | tf_op jit(solution)/shard_map/all_to_all | solution.py:294
  170.6 12.2 %all_to_all.20 = bf16[4,32,1792]{2,1,0:T(8,128)(2,1)S(1)} all-to-all(bf16[4,32,1792]{2,1,0:T(8,128)(2,1)S(1)} %maximum_maximum_fusion), channel_id=1, replica_groups=mesh['x'=4,'zl'=2,'zh'=2,'y'=4,'c'=2] {'x'}, dimensions={0} | all-to-all | bytes 917504 | tf_op jit(solution)/shard_map/all_to_all | solution.py:312
  (100 shorter events, 39.3 us)
Async XLA Ops:
  6.5 66.3 %all-gather.4.cloned.1.call-start = ((), (), s32[]{:S(2)}) async-start(), calls=%async_computation.4 | async-start | bytes 5505024 | tf_op jit(solution)/shard_map/all_gather | solution.py:248
  7.7 15.7 %collective-permute-start.3 = (bf16[2,576,128]{2,1,0:T(8,128)(2,1)S(1)}, bf16[2,576,128]{2,1,0:T(8,128)(2,1)}, u32[]{:S(2)}, u32[]{:S(2)}) collective-permute-start(bf16[2,576,128]{2,1,0:T(8,128)(2,1)S(1)} %pad_maximum_fusion.3), channel_id=1, source_target_pairs={{0,96},{1,112},{16,97},{17,113},{32,0},{33,16},{48,1},{49,17},{64,... | collective-permute-start | bytes 884744 | tf_op jit(solution)/shard_map/ppermute | solution.py:258
  10.6 13.9 %collective-permute-start.2 = (bf16[2,576,128]{2,1,0:T(8,128)(2,1)S(1)}, bf16[2,576,128]{2,1,0:T(8,128)(2,1)}, u32[]{:S(2)}, u32[]{:S(2)}) collective-permute-start(bf16[2,576,128]{2,1,0:T(8,128)(2,1)S(1)} %pad_maximum_fusion.3), channel_id=1, source_target_pairs={{0,64},{1,80},{16,65},{17,81},{32,96},{33,112},{48,97},{49,113},{6... | collective-permute-start | bytes 884744 | tf_op jit(solution)/shard_map/ppermute | solution.py:258
  11.4 16.6 %collective-permute-start.1 = (bf16[2,576,128]{2,1,0:T(8,128)(2,1)S(1)}, bf16[2,576,128]{2,1,0:T(8,128)(2,1)S(1)}, u32[]{:S(2)}, u32[]{:S(2)}) collective-permute-start(bf16[2,576,128]{2,1,0:T(8,128)(2,1)S(1)} %pad_maximum_fusion.3), channel_id=1, source_target_pairs={{0,32},{1,48},{16,33},{17,49},{32,64},{33,80},{48,65},{49,81},{64,... | collective-permute-start | bytes 884744 | tf_op jit(solution)/shard_map/ppermute | solution.py:258
  12.3 15.7 %collective-permute-start = (bf16[2,576,128]{2,1,0:T(8,128)(2,1)S(1)}, bf16[2,576,128]{2,1,0:T(8,128)(2,1)S(1)}, u32[]{:S(2)}, u32[]{:S(2)}) collective-permute-start(bf16[2,576,128]{2,1,0:T(8,128)(2,1)S(1)} %pad_maximum_fusion.3), channel_id=1, source_target_pairs={{0,0},{1,16},{16,1},{17,17},{32,32},{33,48},{48,33},{49,49},{64,64... | collective-permute-start | bytes 884744 | tf_op jit(solution)/shard_map/ppermute | solution.py:258
  13.0 113.8 %all-gather.6.cloned.1.call-start = ((), (), s32[]{:S(2)}) async-start(), calls=%async_computation.5 | async-start | bytes 2621440 | tf_op jit(solution)/shard_map/all_gather | solution.py:290
  28.4 13.4 %collective-permute-start.6 = (bf16[512,384]{1,0:T(8,128)(2,1)S(1)}, bf16[512,384]{1,0:T(8,128)(2,1)S(1)}, u32[]{:S(2)}, u32[]{:S(2)}) collective-permute-start(bf16[512,384]{1,0:T(8,128)(2,1)S(1)} %copy-done.16), channel_id=1, source_target_pairs={{0,32},{32,64},{64,96},{96,0},{1,33},{33,65},{65,97},{97,1},{2,34}... | collective-permute-start | bytes 1179656 | tf_op jit(solution)/shard_map/ppermute | solution.py:27
  28.5 20.6 %collective-permute-start.7 = (bf16[512,384]{1,0:T(8,128)(2,1)S(1)}, bf16[512,384]{1,0:T(8,128)(2,1)S(1)}, u32[]{:S(2)}, u32[]{:S(2)}) collective-permute-start(bf16[512,384]{1,0:T(8,128)(2,1)S(1)} %copy-done.15), channel_id=1, source_target_pairs={{0,64},{32,96},{64,0},{96,32},{1,65},{33,97},{65,1},{97,33},{2,66}... | collective-permute-start | bytes 1179656 | tf_op jit(solution)/shard_map/ppermute | solution.py:27
  31.5 19.1 %collective-permute-start.4 = (bf16[4,576,128]{2,1,0:T(8,128)(2,1)S(1)}, bf16[4,576,128]{2,1,0:T(8,128)(2,1)}, u32[]{:S(2)}, u32[]{:S(2)}) collective-permute-start(bf16[4,576,128]{2,1,0:T(8,128)(2,1)S(1)} %get-tuple-element.45.refs_0_), channel_id=1, source_target_pairs={{0,2},{2,4},{4,6},{6,0},{1,3},{3,5},{5,7},{7,1},{8,10},{10,12},{12... | collective-permute-start | bytes 1769480 | tf_op jit(solution)/shard_map/ppermute | solution.py:27
  33.1 17.5 %collective-permute-start.5 = (bf16[4,576,128]{2,1,0:T(8,128)(2,1)S(1)}, bf16[4,576,128]{2,1,0:T(8,128)(2,1)}, u32[]{:S(2)}, u32[]{:S(2)}) collective-permute-start(bf16[4,576,128]{2,1,0:T(8,128)(2,1)S(1)} %get-tuple-element.45.refs_0_), channel_id=1, source_target_pairs={{0,6},{2,0},{4,2},{6,4},{1,7},{3,1},{5,3},{7,5},{8,14},{10,8},{12,... | collective-permute-start | bytes 1769480 | tf_op jit(solution)/shard_map/ppermute | solution.py:27
  34.8 15.8 %collective-permute-start.8 = (bf16[512,384]{1,0:T(8,128)(2,1)}, bf16[512,384]{1,0:T(8,128)(2,1)}, u32[]{:S(2)}, u32[]{:S(2)}) collective-permute-start(bf16[512,384]{1,0:T(8,128)(2,1)} %get-tuple-element.48), channel_id=1, source_target_pairs={{0,96},{32,0},{64,32},{96,64},{1,97},{33,1},{65,33},{97,65},{2,98}... | collective-permute-start | bytes 1179656 | tf_op jit(solution)/shard_map/ppermute | solution.py:27
  42.5 8.6 %collective-permute-start.11 = (bf16[4,576,128]{2,1,0:T(8,128)(2,1)S(1)}, bf16[4,576,128]{2,1,0:T(8,128)(2,1)}, u32[]{:S(2)}, u32[]{:S(2)}) collective-permute-start(bf16[4,576,128]{2,1,0:T(8,128)(2,1)S(1)} %get-tuple-element.45.refs_0_), channel_id=1, source_target_pairs={{0,1},{1,0},{2,3},{3,2},{4,5},{5,4},{6,7},{7,6},{8,9},{9,8},{10,11... | collective-permute-start | bytes 1769480 | tf_op jit(solution)/shard_map/ppermute | solution.py:27
  50.6 6.2 %collective-permute-start.9 = (bf16[4,576,128]{2,1,0:T(8,128)(2,1)}, bf16[4,576,128]{2,1,0:T(8,128)(2,1)S(1)}, u32[]{:S(2)}, u32[]{:S(2)}) collective-permute-start(bf16[4,576,128]{2,1,0:T(8,128)(2,1)} %collective-permute-done.4.refs_0_), channel_id=1, source_target_pairs={{0,1},{1,0},{2,3},{3,2},{4,5},{5,4},{6,7},{7,6},{8,9},{9,8},{10,11... | collective-permute-start | bytes 1769480 | tf_op jit(solution)/shard_map/ppermute | solution.py:27
  50.7 6.1 %collective-permute-start.10 = (bf16[4,576,128]{2,1,0:T(8,128)(2,1)}, bf16[4,576,128]{2,1,0:T(8,128)(2,1)S(1)}, u32[]{:S(2)}, u32[]{:S(2)}) collective-permute-start(bf16[4,576,128]{2,1,0:T(8,128)(2,1)} %collective-permute-done.5.refs_1_), channel_id=1, source_target_pairs={{0,1},{1,0},{2,3},{3,2},{4,5},{5,4},{6,7},{7,6},{8,9},{9,8},{10,11... | collective-permute-start | bytes 1769480 | tf_op jit(solution)/shard_map/ppermute | solution.py:27
  72.9 27.7 %collective-permute-start.18 = (bf16[1024,1792]{1,0:T(8,128)(2,1)}, bf16[1024,1792]{1,0:T(8,128)(2,1)}, u32[]{:S(2)}, u32[]{:S(2)}) collective-permute-start(bf16[1024,1792]{1,0:T(8,128)(2,1)} %all-gather.4.cloned.1.call-done.refs_4_.refs_1_), channel_id=1, source_target_pairs={{0,1},{1,0},{2,3},{3,2},{4,5},{5,4},{6,7},{7,6},{8,9},{9,8},{10,11... | collective-permute-start | bytes 11010056 | tf_op jit(solution)/shard_map/ppermute | solution.py:27
  73.3 26.7 %collective-permute-start.14 = (bf16[512,512]{1,0:T(8,128)(2,1)}, bf16[512,512]{1,0:T(8,128)(2,1)}, u32[]{:S(2)}, u32[]{:S(2)}) collective-permute-start(bf16[512,512]{1,0:T(8,128)(2,1)} %pad_maximum_fusion.2.refs_0_), channel_id=1, source_target_pairs={{0,32},{32,64},{64,96},{96,0},{1,33},{33,65},{65,97},{97,1},{2,34}... | collective-permute-start | bytes 1572872 | tf_op jit(solution)/shard_map/ppermute | solution.py:27
  73.3 26.7 %collective-permute-start.15 = (bf16[512,512]{1,0:T(8,128)(2,1)}, bf16[512,512]{1,0:T(8,128)(2,1)}, u32[]{:S(2)}, u32[]{:S(2)}) collective-permute-start(bf16[512,512]{1,0:T(8,128)(2,1)} %pad_maximum_fusion.2.refs_0_), channel_id=1, source_target_pairs={{0,64},{32,96},{64,0},{96,32},{1,65},{33,97},{65,1},{97,33},{2,66}... | collective-permute-start | bytes 1572872 | tf_op jit(solution)/shard_map/ppermute | solution.py:27
  75.8 24.8 %collective-permute-start.16 = (bf16[512,512]{1,0:T(8,128)(2,1)}, bf16[512,512]{1,0:T(8,128)(2,1)}, u32[]{:S(2)}, u32[]{:S(2)}) collective-permute-start(bf16[512,512]{1,0:T(8,128)(2,1)} %pad_maximum_fusion.2.refs_0_), channel_id=1, source_target_pairs={{0,96},{32,0},{64,32},{96,64},{1,97},{33,1},{65,33},{97,65},{2,98}... | collective-permute-start | bytes 1572872 | tf_op jit(solution)/shard_map/ppermute | solution.py:27
  108.9 27.4 %all-to-all-start = ((bf16[4,128,1792]{2,1,0:T(8,128)(2,1)}), bf16[4,128,1792]{2,1,0:T(8,128)(2,1)}, u32[]{:S(2)}, u32[]{:S(2)}) async-start(bf16[4,128,1792]{2,1,0:T(8,128)(2,1)} %project_0.1), calls=%async_computation | async-start | bytes 3670016 | tf_op jit(solution)/shard_map/all_to_all | solution.py:305
  136.3 15.6 %collective-permute-start.21 = (bf16[4,64,896]{2,1,0:T(8,128)(2,1)}, bf16[4,64,896]{2,1,0:T(8,128)(2,1)}, u32[]{:S(2)}, u32[]{:S(2)}) collective-permute-start(bf16[4,64,896]{2,1,0:T(8,128)(2,1)} %get-tuple-element.84), channel_id=1, source_target_pairs={{0,8},{8,0},{1,9},{9,1},{2,10},{10,2},{3,11},{11,3},{4,12},{12,4},... | collective-permute-start | bytes 1376264 | tf_op jit(solution)/shard_map/ppermute | solution.py:27
  141.1 15.5 %all-to-all-start.1 = ((bf16[4,128,896]{2,1,0:T(8,128)(2,1)}), bf16[4,128,896]{2,1,0:T(8,128)(2,1)S(1)}, u32[]{:S(2)}, u32[]{:S(2)}) async-start(bf16[4,128,896]{2,1,0:T(8,128)(2,1)} %get-tuple-element.82), calls=%async_computation.1 | async-start | bytes 1835008 | tf_op jit(solution)/shard_map/all_to_all | solution.py:294
  147.1 16.9 %collective-permute-start.19 = (bf16[2,32,1792]{2,1,0:T(8,128)(2,1)}, bf16[2,32,1792]{2,1,0:T(8,128)(2,1)}, u32[]{:S(2)}, u32[]{:S(2)}) collective-permute-start(bf16[2,32,1792]{2,1,0:T(8,128)(2,1)} %dynamic-slice_bitcast_fusion), channel_id=1, source_target_pairs={{0,8},{8,0},{1,9},{9,1},{2,10},{10,2},{3,11},{11,3},{4,12},{12,4},... | collective-permute-start | bytes 688136 | tf_op jit(solution)/shard_map/ppermute | solution.py:27
  156.6 11.9 %all-to-all-start.2 = ((bf16[4,64,896]{2,1,0:T(8,128)(2,1)}), bf16[4,64,896]{2,1,0:T(8,128)(2,1)}, u32[]{:S(2)}, u32[]{:S(2)}) async-start(bf16[4,64,896]{2,1,0:T(8,128)(2,1)} %add_convert_fusion), calls=%async_computation.2 | async-start | bytes 917504 | tf_op jit(solution)/shard_map/all_to_all | solution.py:294
  162.5 7.1 %collective-permute-start.20 = (bf16[2,32,896]{2,1,0:T(8,128)(2,1)S(1)}, bf16[2,32,896]{2,1,0:T(8,128)(2,1)S(1)}, u32[]{:S(2)}, u32[]{:S(2)}) collective-permute-start(bf16[2,32,896]{2,1,0:T(8,128)(2,1)S(1)} %dynamic-slice_bitcast_fusion.3), channel_id=1, source_target_pairs={{0,8},{8,0},{1,9},{9,1},{2,10},{10,2},{3,11},{11,3},{4,12},{12,4},... | collective-permute-start | bytes 344072 | tf_op jit(solution)/shard_map/ppermute | solution.py:27
  (21 other events, 122.0 us)
Sparse Core Ops, SparseCore 0:
  13.2 58.1 all-gather.3
  92.7 34.0 all-gather.5

commit v3 on v2

--- a/solution.py
+++ b/solution.py
@@ -21,6 +21,7 @@
 NT = (((1,), (1,)), ((), ()))
 VMEM = pl.BlockSpec(memory_space=pltpu.VMEM)
 SMEM = pl.BlockSpec(memory_space=pltpu.SMEM)
+ANY = pl.BlockSpec(memory_space=pl.ANY)
 
 
 def shift(a, axis, size, step):
@@ -180,61 +181,84 @@
     )(info, order, *qs, k, v)
 
 
-def project_kernel(split, info, *refs):
-    outs = refs[-3:] if split else refs[-1:]
-    refs = refs[: -len(outs)]
-    ctx, (w_ref, w_far) = refs[:-2], refs[-2:]
-    if len(ctx) == 1:
-        pieces, starts = [ctx[0][n] for n in range(NX)], [256 * n for n in range(NX)]
-    else:
-        pieces = [ref[...] for ref in ctx]
-        starts = [pl.multiple_of(lax.rem(info[0] - s + NX, NX) * 256, 256) for s in range(NX)]
-    left = jnp.concatenate(pieces, axis=1)
-    right = jnp.concatenate([ref[pl.ds(at, 256), :] for at in starts for ref in (w_ref, w_far)], axis=0)
+def project_kernel(info, c0, c1, c2, c3, w_ref, w_far, out_ref):
+    starts = [pl.multiple_of(lax.rem(info[0] - s + NX, NX) * 256, 256) for s in range(NX)]
+    left = jnp.concatenate([ref[...] for ref in (c0, c1, c2, c3)], axis=1)
+    right = jnp.concatenate([ref[0, pl.ds(at, 256), :] for at in starts for ref in (w_ref, w_far)], axis=0)
     out = jnp.dot(left, right, preferred_element_type=F32).astype(BF16)
-
-    def by_y(ref):
+    for y in range(NY):
+        out_ref[y] = out[128 * y : 128 * (y + 1)]
+
+
+def project(info, ctx, w, w_far):
+    width = COLS // 2
+    whole = pl.BlockSpec((512, 512), lambda n: (0, 0))
+    column = pl.BlockSpec((1, 1024, width), lambda n: (n, 0, 0))
+    return pl.pallas_call(
+        project_kernel,
+        out_shape=jax.ShapeDtypeStruct((NY, 128, COLS), BF16),
+        grid=(2,),
+        in_specs=[SMEM] + [whole] * NX + [column, column],
+        out_specs=pl.BlockSpec((NY, 128, width), lambda n: (0, 0, n)),
+        compiler_params=params(56),
+        cost_estimate=cost(4 * 10**10, 7 * 10**6),
+        name="project_0",
+    )(info, *ctx, w, w_far)
+
+
+def fetch_kernel(tie, w_hbm, far_hbm, w_ref, far_ref, done_ref, sems):
+    del tie
+    done_ref[...] = jnp.zeros(done_ref.shape, F32)
+    copies = [pltpu.make_async_copy(w_hbm, w_ref, sems.at[0]), pltpu.make_async_copy(far_hbm, far_ref, sems.at[1])]
+    for copy in copies:
+        copy.start()
+    for copy in copies:
+        copy.wait()
+
+
+def fetch(tie, w, w_far):
+    return pl.pallas_call(
+        fetch_kernel,
+        out_shape=[jax.ShapeDtypeStruct(w.shape, BF16)] * 2 + [jax.ShapeDtypeStruct((8, 128), F32)],
+        in_specs=[SMEM, ANY, ANY],
+        out_specs=[VMEM] * 3,
+        scratch_shapes=[pltpu.SemaphoreType.DMA((2,))],
+        compiler_params=params(16),
+        cost_estimate=cost(4 * 10**9, 7 * 10**6),
+        name="fetch_weights",
+    )(tie, w, w_far)
+
+
+def project_split_kernel(info, ctx, w_ref, w_far, left_ref, keep_ref, give_ref):
+    left = jnp.concatenate([ctx[n] for n in range(NX)], axis=1)
+    for n in range(2):
+        right = jnp.concatenate(
+            [ref[n, 256 * i : 256 * (i + 1), :] for i in range(NX) for ref in (w_ref, w_far)], axis=0
+        )
+        out = jnp.dot(left, right, preferred_element_type=F32).astype(BF16)
         for y in range(NY):
-            ref[y] = out[128 * y : 128 * (y + 1)]
-
-    if not split:
-        by_y(outs[0])
-        return
-
-    @pl.when(pl.program_id(0) == 0)
-    def _():
-        by_y(outs[0])
-
-    @pl.when(pl.program_id(0) == 1)
-    def _():
-        for y in range(NY):
-            for n in range(2):
-                at, rows = 128 * y + 64 * n, slice(32 * n, 32 * (n + 1))
+            if n == 0:
+                left_ref[y] = out[128 * y : 128 * (y + 1)]
+                continue
+            for i in range(2):
+                at, rows = 128 * y + 64 * i, slice(32 * i, 32 * (i + 1))
                 low, high = out[at : at + 32], out[at + 32 : at + 64]
-                outs[1][y, rows] = jnp.where(info[4] == 0, low, high)
-                outs[2][y, rows] = jnp.where(info[4] == 0, high, low)
-
-
-def project(j, info, ctx, w, w_far, split):
+                keep_ref[y, rows] = jnp.where(info[4] == 0, low, high)
+                give_ref[y, rows] = jnp.where(info[4] == 0, high, low)
+
+
+def project_split(info, ctx, w, w_far):
     width = COLS // 2
-    whole = [pl.BlockSpec(a.shape, lambda n, rank=a.ndim: (0,) * rank) for a in ctx]
-    column = pl.BlockSpec((1024, width), lambda n: (0, n))
-    if split:
-        shapes = [(NY, 128, width), (NY, 64, width), (NY, 64, width)]
-        out_specs = [pl.BlockSpec(a, lambda n, rank=len(a): (0,) * rank) for a in shapes]
-    else:
-        shapes = [(NY, 128, COLS)]
-        out_specs = [pl.BlockSpec((NY, 128, width), lambda n: (0, 0, n))]
-    return pl.pallas_call(
-        functools.partial(project_kernel, split),
+    shapes = [(NY, 128, width), (NY, 64, width), (NY, 64, width)]
+    return pl.pallas_call(
+        project_split_kernel,
         out_shape=[jax.ShapeDtypeStruct(a, BF16) for a in shapes],
-        grid=(2,),
-        in_specs=[SMEM] + whole + [column, column],
-        out_specs=out_specs,
-        compiler_params=params(56),
-        cost_estimate=cost(4 * 10**9 if split else 4 * 10**10, 7 * 10**6),
-        name=f"project_{j}",
-    )(info, *ctx, w, w_far)
+        in_specs=[SMEM] + [VMEM] * 3,
+        out_specs=[VMEM] * 3,
+        compiler_params=params(20),
+        cost_estimate=cost(4 * 10**9, 7 * 10**6),
+        name="project_1",
+    )(info, ctx, w, w_far)
 
 
 def hold(*values):
@@ -245,7 +269,7 @@
     x, zl, zh = lax.axis_index("x"), lax.axis_index("zl"), lax.axis_index("zh")
     y, c = lax.axis_index("y"), lax.axis_index("c")
     info = jnp.stack([x, zl, y, c, zh]).astype(jnp.int32)
-    w = lax.all_gather(w_out, "zl", axis=1, tiled=True)
+    w = lax.all_gather(w_out, "zl", axis=0, tiled=False)
 
     columns = latents.T
 
@@ -301,10 +325,12 @@
         pick = lambda n: lax.dynamic_index_in_dim(a, n, 1, keepdims=False)
         return pick(zh), pick(1 - zh)
 
-    (p0,) = project(0, info3, g0, w, w_far, False)
+    p0 = project(info3, g0, w, w_far)
     y0 = lax.all_to_all(p0, "y", 0, 0, tiled=True)
-    p0, g1, info4 = hold(p0, g1, info3)
-    left, keep, give, y0 = hold(*project(1, info4, [g1], w, w_far, True), y0)
+    p0, info5 = hold(p0, info3)
+    w, w_far, done = fetch(info5, w, w_far)
+    g1, info4 = hold(g1, info5 + done[0, : info.size].astype(jnp.int32))
+    left, keep, give, y0 = hold(*project_split(info4, g1, w, w_far), y0)
     left, right = over_y(left), over_z(keep, give)
     left, right = over_z(*halves(left)), over_y(right).reshape(2, 32, COLS // 2)
     s0 = over_z(*halves(add_up(y0)))

time: 192 us -> 192 us (level); the launches traced: 190 us -> 193 us
  waiting for transfers between devices: 59 us -> 45.5 us
  local copies, waits for them, and re-layouts: 16.7 us -> 27.2 us
  Pallas kernels: 43.4 us -> 48.9 us
  starting transfers between devices: 36.5 us -> 39.6 us
    unnamed x38 -> x56, local copies, waits for them, and re-layouts: 8.17 us -> 19.6 us
    all_gather x1, waiting for transfers between devices: 13.4 us -> 5.16 us  [on_device(): g1 = lax.all_gather(a1, 'x', axis=0, tiled=False)]
    pallas_call x2, Pallas kernels: 19.4 us -> 25.7 us  [attend(): pl.pallas_call(functools.partial(attend_kernel, j), out_shape=(half, half...]
    ppermute x4, waiting for transfers between devices: 9.15 us -> 5.41 us  [across(): return lax.ppermute(part, ('x', 'zl', 'c'), pairs)]
    pallas_call x2 -> x3, Pallas kernels: 17.1 us -> 16.3 us  [the longest x1 8.38 us: project(): pl.pallas_call(project_kernel, out_shape=jax.ShapeDtypeStruct((NY, 128, C...]
  transfers between devices with their start and end apart: 27 -> 27, of which waited for: 14 -> 12; matrix products, arithmetic and copies ran while one was open for 8% -> 7% of each run, Pallas kernels for 23% -> 25%
where the time goes in v3:
time: 192 us; the launch traced here: 193 us
  Pallas kernels  48.9 us (25%)
  waiting for transfers between devices  45.5 us (24%)
  starting transfers between devices  39.6 us (21%)
  local copies, waits for them, and re-layouts  27.2 us (14%)
  between operations  13.9 us (7%)
  blocking collectives  10.6 us (6%)
  other arithmetic  7.21 us (4%)
    ppermute x18, waiting for transfers between devices, shift(): return lax.ppermute(a, axis, [(i, (i + step) % size) for i in range(size)])  29.8 us
    pallas_call x2, Pallas kernels, attend(): pl.pallas_call(functools.partial(attend_kernel, j), out_shape=(half, half...  25.7 us
    ppermute x18, starting transfers between devices, shift(): return lax.ppermute(a, axis, [(i, (i + step) % size) for i in range(size)])  20.1 us
    unnamed x56, local copies, waits for them, and re-layouts  19.6 us
    all_to_all x1, blocking collectives, on_device(): out = lax.all_to_all(total, 'x', 0, 0, tiled=True)  10.6 us
    pallas_call x1, Pallas kernels, project(): pl.pallas_call(project_kernel, out_shape=jax.ShapeDtypeStruct((NY, 128, C...  8.38 us
    all_to_all x2, starting transfers between devices, over_y(): return add_up(lax.all_to_all(a, 'y', 0, 0, tiled=True))  7.75 us
    ppermute x4, starting transfers between devices, across(): return lax.ppermute(part, ('x', 'zl', 'c'), pairs)  7.11 us
  transfers between devices with their start and end apart: 27, of which 12 were waited for; matrix products, arithmetic and copies ran while one was open for 7% of the time, Pallas kernels for 25%

profile of v3, /device:TPU:0, one launch (start us, length us, event | category | flops | bytes accessed | tf_op | source)
XLA Modules:
  0.0 192.9 jit_solution(16601085162946660779)
XLA Ops:
  10.7 2.7 %collective-permute-start.2 = (bf16[2,576,128]{2,1,0:T(8,128)(2,1)S(1)}, bf16[2,576,128]{2,1,0:T(8,128)(2,1)S(1)}, u32[]{:S(2)}, u32[]{:S(2)}) collective-permute-start(bf16[2,576,128]{2,1,0:T(8,128)(2,1)S(1)} %pad_maximum_fusion.3), channel_id=1, source_target_pairs={{0,64},{1,80},{16,65},{17,81},{32,96},{33,112},{48,97},{49,113},{6... | collective-permute-start | bytes 884744 | tf_op jit(solution)/shard_map/ppermute | solution.py:282
  15.0 2.6 %constant_dynamic-slice_fusion.1 = (bf16[512,384]{1,0:T(8,128)(2,1)}, bf16[512,384]{1,0:T(8,128)(2,1)}, bf16[512,384]{1,0:T(8,128)(2,1)}, bf16[512,384]{1,0:T(8,128)(2,1)}) fusion(bf16[512,1536]{1,0:T(8,128)(2,1)} %param.6, s32[]{:T(128)S(6)} %select_n.64, s32[]{:T(128)S(6)} %select_n.60, s32[]{:T(128)S(6)} %select_n.58, s32[]{:T(128)S(6)} %select_n.62), kind=kLoop, calls=%fused_computation.17 | loop fusion | bytes 3145744 | tf_op jit(solution)/shard_map/dynamic_slice | solution.py:291
  20.7 5.4 %collective-permute-done.2 = bf16[2,576,128]{2,1,0:T(8,128)(2,1)S(1)} collective-permute-done((bf16[2,576,128]{2,1,0:T(8,128)(2,1)S(1)}, bf16[2,576,128]{2,1,0:T(8,128)(2,1)S(1)}, u32[]{:S(2)}, u32[]{:S(2)}) %collective-permute-start.2) | collective-permute-done | bytes 294944 | tf_op jit(solution)/shard_map/ppermute | solution.py:282
  26.5 2.7 %collective-permute-start.6 = (bf16[512,384]{1,0:T(8,128)(2,1)S(1)}, bf16[512,384]{1,0:T(8,128)(2,1)S(1)}, u32[]{:S(2)}, u32[]{:S(2)}) collective-permute-start(bf16[512,384]{1,0:T(8,128)(2,1)S(1)} %copy-done.25), channel_id=1, source_target_pairs={{0,32},{32,64},{64,96},{96,0},{1,33},{33,65},{65,97},{97,1},{2,34}... | collective-permute-start | bytes 1179656 | tf_op jit(solution)/shard_map/ppermute | solution.py:28
  35.2 2.6 %collective-permute-done.6.q1 = bf16[512,384]{1,0:T(8,128)(2,1)S(1)} collective-permute-done((bf16[512,384]{1,0:T(8,128)(2,1)S(1)}, bf16[512,384]{1,0:T(8,128)(2,1)S(1)}, u32[]{:S(2)}, u32[]{:S(2)}) %collective-permute-start.6) | collective-permute-done | bytes 393248 | tf_op jit(solution)/shard_map/ppermute | solution.py:28
  38.5 2.6 %collective-permute-start.11 = (bf16[4,576,128]{2,1,0:T(8,128)(2,1)S(1)}, bf16[4,576,128]{2,1,0:T(8,128)(2,1)}, u32[]{:S(2)}, u32[]{:S(2)}) collective-permute-start(bf16[4,576,128]{2,1,0:T(8,128)(2,1)S(1)} %get-tuple-element.49.refs_0_), channel_id=1, source_target_pairs={{0,1},{1,0},{2,3},{3,2},{4,5},{5,4},{6,7},{7,6},{8,9},{9,8},{10,11... | collective-permute-start | bytes 1769480 | tf_op jit(solution)/shard_map/ppermute | solution.py:28
  41.1 8.6 %collective-permute-done.7.q2 = bf16[512,384]{1,0:T(8,128)(2,1)S(1)} collective-permute-done((bf16[512,384]{1,0:T(8,128)(2,1)S(1)}, bf16[512,384]{1,0:T(8,128)(2,1)S(1)}, u32[]{:S(2)}, u32[]{:S(2)}) %collective-permute-start.7) | collective-permute-done | bytes 393248 | tf_op jit(solution)/shard_map/ppermute | solution.py:28
  53.7 3.4 %keys_values_0.1 = (bf16[2,256,4096]{2,1,0:T(8,128)(2,1)S(1)}, bf16[2,128,4096]{2,1,0:T(8,128)(2,1)S(1)}) custom-call(s32[5]{0:T(128)S(1)} %stack.43.info.tie, s32[16]{0:T(128)S(1)} %copy-done.14, bf16[4,576,128]{2,1,0:T(8,128)(2,1)S(1)} %get-tuple-element.49.refs_0_, bf16[4,576,128]{2,1,0:T(8,128)(2,1)S(1)} %get-tuple-element.62.refs_1_, ...), custom_call_target="tpu_custom_call" | custom-call | flops 3000000000 | bytes 5000000 | tf_op jit(solution)/shard_map/keys_values_0/pallas_call | solution.py:69
  57.2 3.5 %keys_values_1.1 = (bf16[2,256,4096]{2,1,0:T(8,128)(2,1)S(1)}, bf16[2,128,4096]{2,1,0:T(8,128)(2,1)S(1)}) custom-call(s32[5]{0:T(128)S(1)} %stack.43.info.tie, s32[16]{0:T(128)S(1)} %copy-done.14, bf16[4,576,128]{2,1,0:T(8,128)(2,1)} %collective-permute-done.4.refs_0_, ...), custom_call_target="tpu_custom_call", output_to_operand_aliasing={{0}: (8, {}), {1}: (9, {})} | custom-call | flops 3000000000 | bytes 5000000 | tf_op jit(solution)/shard_map/keys_values_1/pallas_call | solution.py:69
  60.7 13.7 %attend_0.1 = (bf16[512,256]{1,0:T(8,128)(2,1)S(1)}, bf16[512,256]{1,0:T(8,128)(2,1)S(1)}) custom-call(s32[5]{0:T(128)S(1)} %stack.43.info.tie, s32[16]{0:T(128)S(1)} %copy-done.14, bf16[512,384]{1,0:T(8,128)(2,1)S(1)} %copy-done.3, bf16[512,384]{1,0:T(8,128)(2,1)S(1)} %copy-done.9, bf16[512,384]{1,0:T(8,128)(2,1)S(1)} %copy-done.12, ...), custom_call_target="tpu_custom_call" | custom-call | flops 10000000000 | bytes 7000000 | tf_op jit(solution)/shard_map/attend_0/pallas_call | solution.py:171
  84.6 12.0 %attend_2.1 = (bf16[512,256]{1,0:T(8,128)(2,1)S(1)}, bf16[512,256]{1,0:T(8,128)(2,1)S(1)}) custom-call(s32[5]{0:T(128)S(1)} %stack.43.info.tie, s32[16]{0:T(128)S(1)} %copy-done.14, bf16[512,384]{1,0:T(8,128)(2,1)S(1)} %copy-done.3, bf16[512,384]{1,0:T(8,128)(2,1)S(1)} %copy-done.10, bf16[512,384]{1,0:T(8,128)(2,1)S(1)} %copy-done.13, ...), custom_call_target="tpu_custom_call" | custom-call | flops 10000000000 | bytes 7000000 | tf_op jit(solution)/shard_map/attend_2/pallas_call | solution.py:171
  99.0 5.0 %collective-permute-done.15.c1 = bf16[512,512]{1,0:T(8,128)(2,1)} collective-permute-done((bf16[512,512]{1,0:T(8,128)(2,1)}, bf16[512,512]{1,0:T(8,128)(2,1)}, u32[]{:S(2)}, u32[]{:S(2)}) %collective-permute-start.15) | collective-permute-done | bytes 524320 | tf_op jit(solution)/shard_map/ppermute | solution.py:28
  104.7 8.4 %project_0.1 = bf16[4,128,1792]{2,1,0:T(8,128)(2,1)} custom-call(s32[5]{0:T(128)} %copy-done.4, bf16[512,512]{1,0:T(8,128)(2,1)} %pad_maximum_fusion.2.c0, bf16[512,512]{1,0:T(8,128)(2,1)} %collective-permute-done.15.c1, bf16[512,512]{1,0:T(8,128)(2,1)} %collective-permute-done.16.c2, bf16[512,512]{1,0:T(8,128)(2,1)} %collective-permute-done.17.c3, ...), custom_call_target="tpu_custom_call" | custom-call | flops 40000000000 | bytes 7000000 | tf_op jit(solution)/shard_map/project_0/pallas_call | solution.py:197
  113.1 4.6 %all-to-all-start = ((bf16[4,128,1792]{2,1,0:T(8,128)(2,1)}), bf16[4,128,1792]{2,1,0:T(8,128)(2,1)}, u32[]{:S(2)}, u32[]{:S(2)}) async-start(bf16[4,128,1792]{2,1,0:T(8,128)(2,1)} %project_0.1), calls=%async_computation | async-start | bytes 3670016 | tf_op jit(solution)/shard_map/all_to_all | solution.py:329
  119.8 2.9 %fetch_weights.1 = (bf16[2,1024,896]{2,1,0:T(8,128)(2,1)S(1)}, bf16[2,1024,896]{2,1,0:T(8,128)(2,1)S(1)}, f32[8,128]{1,0:T(8,128)S(1)}) custom-call(s32[5]{0:T(128)S(1)} %copy-done.5, bf16[2,1024,896]{2,1,0:T(8,128)(2,1)S(1)} %bitcast.40, bf16[2,1024,896]{2,1,0:T(8,128)(2,1)} %collective-permute-done.18.w_far.far_hbm), custom_call_target="tpu_custom_call" | custom-call | flops 4000000000 | bytes 7000000 | tf_op jit(solution)/shard_map/fetch_weights/pallas_call | solution.py:220
  126.3 5.2 %all-gather.7.cloned.1.call-done = bf16[2048,512]{1,0:T(8,128)(2,1)} async-done(((bf16[512,512]{1,0:T(8,128)(2,1)}), bf16[2048,512]{1,0:T(8,128)(2,1)}) %all-gather.7.cloned.1.call-update) | async-done | bytes 2097168 | tf_op jit(solution)/shard_map/all_gather | solution.py:314
  137.1 5.0 %project_1.1 = (bf16[4,128,896]{2,1,0:T(8,128)(2,1)}, bf16[4,64,896]{2,1,0:T(8,128)(2,1)S(1)}, bf16[4,64,896]{2,1,0:T(8,128)(2,1)S(1)}) custom-call(s32[5]{0:T(128)S(1)} %bitcast_add_fusion.info, bf16[4,512,512]{2,1,0:T(8,128)(2,1)S(1)} %bitcast.41, bf16[2,1024,896]{2,1,0:T(8,128)(2,1)S(1)} %copy-done.20, bf16[2,1024,896]{2,1,0:T(8,128)(2,1)S(1)} %copy-done.22), custom_call_target="tpu_custom_call" | custom-call | flops 4000000000 | bytes 7000000 | tf_op jit(solution)/shard_map/project_1/pallas_call | solution.py:253
  142.1 3.2 %collective-permute-start.21 = (bf16[4,64,896]{2,1,0:T(8,128)(2,1)S(1)}, bf16[4,64,896]{2,1,0:T(8,128)(2,1)}, u32[]{:S(2)}, u32[]{:S(2)}) collective-permute-start(bf16[4,64,896]{2,1,0:T(8,128)(2,1)S(1)} %get-tuple-element.92), channel_id=1, source_target_pairs={{0,8},{8,0},{1,9},{9,1},{2,10},{10,2},{3,11},{11,3},{4,12},{12,4},... | collective-permute-start | bytes 1376264 | tf_op jit(solution)/shard_map/ppermute | solution.py:28
  145.4 4.3 %all-to-all-start.1 = ((bf16[4,128,896]{2,1,0:T(8,128)(2,1)}), bf16[4,128,896]{2,1,0:T(8,128)(2,1)}, u32[]{:S(2)}, u32[]{:S(2)}) async-start(bf16[4,128,896]{2,1,0:T(8,128)(2,1)} %get-tuple-element.90), calls=%async_computation.1 | async-start | bytes 1835008 | tf_op jit(solution)/shard_map/all_to_all | solution.py:318
  152.6 3.7 %collective-permute-done.21 = bf16[4,64,896]{2,1,0:T(8,128)(2,1)} collective-permute-done((bf16[4,64,896]{2,1,0:T(8,128)(2,1)S(1)}, bf16[4,64,896]{2,1,0:T(8,128)(2,1)}, u32[]{:S(2)}, u32[]{:S(2)}) %collective-permute-start.21) | collective-permute-done | bytes 458784 | tf_op jit(solution)/shard_map/ppermute | solution.py:28
  158.2 5.1 %all-to-all-done.1 = bf16[4,128,896]{2,1,0:T(8,128)(2,1)} async-done(((bf16[4,128,896]{2,1,0:T(8,128)(2,1)}), bf16[4,128,896]{2,1,0:T(8,128)(2,1)}, u32[]{:S(2)}, u32[]{:S(2)}) %all-to-all-start.1) | async-done | bytes 917536 | tf_op jit(solution)/shard_map/all_to_all | solution.py:318
  163.3 3.5 %all-to-all-start.2 = ((bf16[4,64,896]{2,1,0:T(8,128)(2,1)}), bf16[4,64,896]{2,1,0:T(8,128)(2,1)S(1)}, u32[]{:S(2)}, u32[]{:S(2)}) async-start(bf16[4,64,896]{2,1,0:T(8,128)(2,1)} %add_convert_fusion), calls=%async_computation.2 | async-start | bytes 917504 | tf_op jit(solution)/shard_map/all_to_all | solution.py:318
  169.6 4.9 %collective-permute-done.20 = bf16[2,32,896]{2,1,0:T(8,128)(2,1)S(1)} collective-permute-done((bf16[2,32,896]{2,1,0:T(8,128)(2,1)S(1)}, bf16[2,32,896]{2,1,0:T(8,128)(2,1)S(1)}, u32[]{:S(2)}, u32[]{:S(2)}) %collective-permute-start.20) | collective-permute-done | bytes 114720 | tf_op jit(solution)/shard_map/ppermute | solution.py:28
  174.7 10.6 %all_to_all.20 = bf16[4,32,1792]{2,1,0:T(8,128)(2,1)S(1)} all-to-all(bf16[4,32,1792]{2,1,0:T(8,128)(2,1)S(1)} %maximum_maximum_fusion), channel_id=1, replica_groups=mesh['x'=4,'zl'=2,'zh'=2,'y'=4,'c'=2] {'x'}, dimensions={0} | all-to-all | bytes 917504 | tf_op jit(solution)/shard_map/all_to_all | solution.py:338
  (120 shorter events, 52.8 us)
Async XLA Ops:
  6.5 70.4 %all-gather.5.cloned.1.call-start = ((), (), s32[]{:S(2)}) async-start(), calls=%async_computation.4 | async-start | bytes 5505024 | tf_op jit(solution)/shard_map/all_gather | solution.py:272
  7.7 10.9 %collective-permute-start = (bf16[2,576,128]{2,1,0:T(8,128)(2,1)S(1)}, bf16[2,576,128]{2,1,0:T(8,128)(2,1)}, u32[]{:S(2)}, u32[]{:S(2)}) collective-permute-start(bf16[2,576,128]{2,1,0:T(8,128)(2,1)S(1)} %pad_maximum_fusion.3), channel_id=1, source_target_pairs={{0,0},{1,16},{16,1},{17,17},{32,32},{33,48},{48,33},{49,49},{64,64... | collective-permute-start | bytes 884744 | tf_op jit(solution)/shard_map/ppermute | solution.py:282
  9.1 10.5 %collective-permute-start.1 = (bf16[2,576,128]{2,1,0:T(8,128)(2,1)S(1)}, bf16[2,576,128]{2,1,0:T(8,128)(2,1)}, u32[]{:S(2)}, u32[]{:S(2)}) collective-permute-start(bf16[2,576,128]{2,1,0:T(8,128)(2,1)S(1)} %pad_maximum_fusion.3), channel_id=1, source_target_pairs={{0,32},{1,48},{16,33},{17,49},{32,64},{33,80},{48,65},{49,81},{64,... | collective-permute-start | bytes 884744 | tf_op jit(solution)/shard_map/ppermute | solution.py:282
  10.7 15.4 %collective-permute-start.2 = (bf16[2,576,128]{2,1,0:T(8,128)(2,1)S(1)}, bf16[2,576,128]{2,1,0:T(8,128)(2,1)S(1)}, u32[]{:S(2)}, u32[]{:S(2)}) collective-permute-start(bf16[2,576,128]{2,1,0:T(8,128)(2,1)S(1)} %pad_maximum_fusion.3), channel_id=1, source_target_pairs={{0,64},{1,80},{16,65},{17,81},{32,96},{33,112},{48,97},{49,113},{6... | collective-permute-start | bytes 884744 | tf_op jit(solution)/shard_map/ppermute | solution.py:282
  13.4 12.7 %collective-permute-start.3 = (bf16[2,576,128]{2,1,0:T(8,128)(2,1)S(1)}, bf16[2,576,128]{2,1,0:T(8,128)(2,1)S(1)}, u32[]{:S(2)}, u32[]{:S(2)}) collective-permute-start(bf16[2,576,128]{2,1,0:T(8,128)(2,1)S(1)} %pad_maximum_fusion.3), channel_id=1, source_target_pairs={{0,96},{1,112},{16,97},{17,113},{32,0},{33,16},{48,1},{49,17},{64,... | collective-permute-start | bytes 884744 | tf_op jit(solution)/shard_map/ppermute | solution.py:282
  14.9 116.5 %all-gather.7.cloned.1.call-start = ((), (), s32[]{:S(2)}) async-start(), calls=%async_computation.5 | async-start | bytes 2621440 | tf_op jit(solution)/shard_map/all_gather | solution.py:314
  26.5 11.3 %collective-permute-start.6 = (bf16[512,384]{1,0:T(8,128)(2,1)S(1)}, bf16[512,384]{1,0:T(8,128)(2,1)S(1)}, u32[]{:S(2)}, u32[]{:S(2)}) collective-permute-start(bf16[512,384]{1,0:T(8,128)(2,1)S(1)} %copy-done.25), channel_id=1, source_target_pairs={{0,32},{32,64},{64,96},{96,0},{1,33},{33,65},{65,97},{97,1},{2,34}... | collective-permute-start | bytes 1179656 | tf_op jit(solution)/shard_map/ppermute | solution.py:28
  29.2 20.6 %collective-permute-start.7 = (bf16[512,384]{1,0:T(8,128)(2,1)S(1)}, bf16[512,384]{1,0:T(8,128)(2,1)S(1)}, u32[]{:S(2)}, u32[]{:S(2)}) collective-permute-start(bf16[512,384]{1,0:T(8,128)(2,1)S(1)} %copy-done.24), channel_id=1, source_target_pairs={{0,64},{32,96},{64,0},{96,32},{1,65},{33,97},{65,1},{97,33},{2,66}... | collective-permute-start | bytes 1179656 | tf_op jit(solution)/shard_map/ppermute | solution.py:28
  31.6 19.0 %collective-permute-start.4 = (bf16[4,576,128]{2,1,0:T(8,128)(2,1)S(1)}, bf16[4,576,128]{2,1,0:T(8,128)(2,1)}, u32[]{:S(2)}, u32[]{:S(2)}) collective-permute-start(bf16[4,576,128]{2,1,0:T(8,128)(2,1)S(1)} %get-tuple-element.49.refs_0_), channel_id=1, source_target_pairs={{0,2},{2,4},{4,6},{6,0},{1,3},{3,5},{5,7},{7,1},{8,10},{10,12},{12... | collective-permute-start | bytes 1769480 | tf_op jit(solution)/shard_map/ppermute | solution.py:28
  33.3 17.2 %collective-permute-start.5 = (bf16[4,576,128]{2,1,0:T(8,128)(2,1)S(1)}, bf16[4,576,128]{2,1,0:T(8,128)(2,1)}, u32[]{:S(2)}, u32[]{:S(2)}) collective-permute-start(bf16[4,576,128]{2,1,0:T(8,128)(2,1)S(1)} %get-tuple-element.49.refs_0_), channel_id=1, source_target_pairs={{0,6},{2,0},{4,2},{6,4},{1,7},{3,1},{5,3},{7,5},{8,14},{10,8},{12,... | collective-permute-start | bytes 1769480 | tf_op jit(solution)/shard_map/ppermute | solution.py:28
  34.9 15.7 %collective-permute-start.8 = (bf16[512,384]{1,0:T(8,128)(2,1)}, bf16[512,384]{1,0:T(8,128)(2,1)}, u32[]{:S(2)}, u32[]{:S(2)}) collective-permute-start(bf16[512,384]{1,0:T(8,128)(2,1)} %get-tuple-element.52), channel_id=1, source_target_pairs={{0,96},{32,0},{64,32},{96,64},{1,97},{33,1},{65,33},{97,65},{2,98}... | collective-permute-start | bytes 1179656 | tf_op jit(solution)/shard_map/ppermute | solution.py:28
  38.5 12.8 %collective-permute-start.11 = (bf16[4,576,128]{2,1,0:T(8,128)(2,1)S(1)}, bf16[4,576,128]{2,1,0:T(8,128)(2,1)}, u32[]{:S(2)}, u32[]{:S(2)}) collective-permute-start(bf16[4,576,128]{2,1,0:T(8,128)(2,1)S(1)} %get-tuple-element.49.refs_0_), channel_id=1, source_target_pairs={{0,1},{1,0},{2,3},{3,2},{4,5},{5,4},{6,7},{7,6},{8,9},{9,8},{10,11... | collective-permute-start | bytes 1769480 | tf_op jit(solution)/shard_map/ppermute | solution.py:28
  50.6 6.5 %collective-permute-start.10 = (bf16[4,576,128]{2,1,0:T(8,128)(2,1)}, bf16[4,576,128]{2,1,0:T(8,128)(2,1)S(1)}, u32[]{:S(2)}, u32[]{:S(2)}) collective-permute-start(bf16[4,576,128]{2,1,0:T(8,128)(2,1)} %collective-permute-done.5.refs_1_), channel_id=1, source_target_pairs={{0,1},{1,0},{2,3},{3,2},{4,5},{5,4},{6,7},{7,6},{8,9},{9,8},{10,11... | collective-permute-start | bytes 1769480 | tf_op jit(solution)/shard_map/ppermute | solution.py:28
  51.2 6.0 %collective-permute-start.9 = (bf16[4,576,128]{2,1,0:T(8,128)(2,1)}, bf16[4,576,128]{2,1,0:T(8,128)(2,1)S(1)}, u32[]{:S(2)}, u32[]{:S(2)}) collective-permute-start(bf16[4,576,128]{2,1,0:T(8,128)(2,1)} %collective-permute-done.4.refs_0_), channel_id=1, source_target_pairs={{0,1},{1,0},{2,3},{3,2},{4,5},{5,4},{6,7},{7,6},{8,9},{9,8},{10,11... | collective-permute-start | bytes 1769480 | tf_op jit(solution)/shard_map/ppermute | solution.py:28
  77.0 27.7 %collective-permute-start.18 = (bf16[2,1024,896]{2,1,0:T(8,128)(2,1)}, bf16[2,1024,896]{2,1,0:T(8,128)(2,1)}, u32[]{:S(2)}, u32[]{:S(2)}) collective-permute-start(bf16[2,1024,896]{2,1,0:T(8,128)(2,1)} %bitcast.38), channel_id=1, source_target_pairs={{0,1},{1,0},{2,3},{3,2},{4,5},{5,4},{6,7},{7,6},{8,9},{9,8},{10,11... | collective-permute-start | bytes 11010056 | tf_op jit(solution)/shard_map/ppermute | solution.py:28
  77.1 27.0 %collective-permute-start.15 = (bf16[512,512]{1,0:T(8,128)(2,1)}, bf16[512,512]{1,0:T(8,128)(2,1)}, u32[]{:S(2)}, u32[]{:S(2)}) collective-permute-start(bf16[512,512]{1,0:T(8,128)(2,1)} %pad_maximum_fusion.2.c0), channel_id=1, source_target_pairs={{0,32},{32,64},{64,96},{96,0},{1,33},{33,65},{65,97},{97,1},{2,34}... | collective-permute-start | bytes 1572872 | tf_op jit(solution)/shard_map/ppermute | solution.py:28
  77.1 27.0 %collective-permute-start.16 = (bf16[512,512]{1,0:T(8,128)(2,1)}, bf16[512,512]{1,0:T(8,128)(2,1)}, u32[]{:S(2)}, u32[]{:S(2)}) collective-permute-start(bf16[512,512]{1,0:T(8,128)(2,1)} %pad_maximum_fusion.2.c0), channel_id=1, source_target_pairs={{0,64},{32,96},{64,0},{96,32},{1,65},{33,97},{65,1},{97,33},{2,66}... | collective-permute-start | bytes 1572872 | tf_op jit(solution)/shard_map/ppermute | solution.py:28
  78.7 26.0 %collective-permute-start.17 = (bf16[512,512]{1,0:T(8,128)(2,1)}, bf16[512,512]{1,0:T(8,128)(2,1)}, u32[]{:S(2)}, u32[]{:S(2)}) collective-permute-start(bf16[512,512]{1,0:T(8,128)(2,1)} %pad_maximum_fusion.2.c0), channel_id=1, source_target_pairs={{0,96},{32,0},{64,32},{96,64},{1,97},{33,1},{65,33},{97,65},{2,98}... | collective-permute-start | bytes 1572872 | tf_op jit(solution)/shard_map/ppermute | solution.py:28
  113.1 29.0 %all-to-all-start = ((bf16[4,128,1792]{2,1,0:T(8,128)(2,1)}), bf16[4,128,1792]{2,1,0:T(8,128)(2,1)}, u32[]{:S(2)}, u32[]{:S(2)}) async-start(bf16[4,128,1792]{2,1,0:T(8,128)(2,1)} %project_0.1), calls=%async_computation | async-start | bytes 3670016 | tf_op jit(solution)/shard_map/all_to_all | solution.py:329
  142.1 14.2 %collective-permute-start.21 = (bf16[4,64,896]{2,1,0:T(8,128)(2,1)S(1)}, bf16[4,64,896]{2,1,0:T(8,128)(2,1)}, u32[]{:S(2)}, u32[]{:S(2)}) collective-permute-start(bf16[4,64,896]{2,1,0:T(8,128)(2,1)S(1)} %get-tuple-element.92), channel_id=1, source_target_pairs={{0,8},{8,0},{1,9},{9,1},{2,10},{10,2},{3,11},{11,3},{4,12},{12,4},... | collective-permute-start | bytes 1376264 | tf_op jit(solution)/shard_map/ppermute | solution.py:28
  145.4 18.0 %all-to-all-start.1 = ((bf16[4,128,896]{2,1,0:T(8,128)(2,1)}), bf16[4,128,896]{2,1,0:T(8,128)(2,1)}, u32[]{:S(2)}, u32[]{:S(2)}) async-start(bf16[4,128,896]{2,1,0:T(8,128)(2,1)} %get-tuple-element.90), calls=%async_computation.1 | async-start | bytes 1835008 | tf_op jit(solution)/shard_map/all_to_all | solution.py:318
  152.2 16.4 %collective-permute-start.19 = (bf16[2,32,1792]{2,1,0:T(8,128)(2,1)}, bf16[2,32,1792]{2,1,0:T(8,128)(2,1)}, u32[]{:S(2)}, u32[]{:S(2)}) collective-permute-start(bf16[2,32,1792]{2,1,0:T(8,128)(2,1)} %dynamic-slice_bitcast_fusion), channel_id=1, source_target_pairs={{0,8},{8,0},{1,9},{9,1},{2,10},{10,2},{3,11},{11,3},{4,12},{12,4},... | collective-permute-start | bytes 688136 | tf_op jit(solution)/shard_map/ppermute | solution.py:28
  163.3 11.2 %all-to-all-start.2 = ((bf16[4,64,896]{2,1,0:T(8,128)(2,1)}), bf16[4,64,896]{2,1,0:T(8,128)(2,1)S(1)}, u32[]{:S(2)}, u32[]{:S(2)}) async-start(bf16[4,64,896]{2,1,0:T(8,128)(2,1)} %add_convert_fusion), calls=%async_computation.2 | async-start | bytes 917504 | tf_op jit(solution)/shard_map/all_to_all | solution.py:318
  168.2 6.4 %collective-permute-start.20 = (bf16[2,32,896]{2,1,0:T(8,128)(2,1)S(1)}, bf16[2,32,896]{2,1,0:T(8,128)(2,1)S(1)}, u32[]{:S(2)}, u32[]{:S(2)}) collective-permute-start(bf16[2,32,896]{2,1,0:T(8,128)(2,1)S(1)} %dynamic-slice_bitcast_fusion.3), channel_id=1, source_target_pairs={{0,8},{8,0},{1,9},{9,1},{2,10},{10,2},{3,11},{11,3},{4,12},{12,4},... | collective-permute-start | bytes 344072 | tf_op jit(solution)/shard_map/ppermute | solution.py:28
  (30 other events, 207.7 us)
Sparse Core Ops, SparseCore 0:
  15.0 55.7 all-gather.4
  99.2 32.2 all-gather.6
